TPU v7x, 128 devices: a whole 4x4x4 slice. The times are simulated.
128 devices in a mesh: wave: 16 (over y_hi, x, core), lev: 8 (over y_lo, z).
Axes of the slice: x: 4, y: 4 (y_hi: 2, y_lo: 2; y = y_hi * 2 + y_lo), z: 4, core: 2. Of those that a mesh axis runs over, the one named last changes fastest.
Arguments:
- spectral: bfloat16 [1280, 2, 2, 64, 1280], P('wave', None, None, 'lev'), may hold values from -0.125 to 0.125
- legendre: bfloat16 [1280, 64, 1280], P('wave'), may hold values from -0.15625 to 0.15625
- derivative: bfloat16 [1280, 64, 1280], P('wave'), may hold values from -0.15625 to 0.15625
- wave_order: int32 [1280], replicated, may hold values from 0 to 1279, each once
- lat_order: int32 [128], replicated, may hold values from 0 to 127, each once
- row_lengths: int32 [64], replicated, may hold values from 20 to 5136, as said below
- tile_map: int32 [48], replicated, may hold values from 0 to 47, each once
Outputs:
- grid: bfloat16 [128, 3, 64, 6144], P('wave', None, None, 'lev')
- vort_max: float32 [], replicated
Inputs may be any that keep to these rules, and one draw needn't show every extreme that they name: `wave_order`: each of 0 to 1279 once. `lat_order`: each of 0 to 127 once. `row_lengths`: each is 4 j + 20 for a whole number j below 1280; the largest, 5136, occurs in every draw. `tile_map`: each of 0 to 47 once.
All inputs are finite; a program needn't handle non-finite values.
Results may differ from a plain program's by a relative error of at most 0.0061.
Values may be sent and summed in bfloat16 or wider, within the bound.
No kernel may reach another device: no remote copies, remote signals or barrier semaphores. Data moves between devices by JAX's collectives and lax.ppermute only.
A program may use at most 192 MiB of HBM per device.

v0:
```python
import functools

import jax
import jax.numpy as jnp
from jax import lax
from jax.experimental import pallas as pl
from jax.experimental.pallas import tpu as pltpu
from jax.sharding import PartitionSpec as P

NM = 1280
TILE = 128
GROUP = 16
SPAN = 256
BLOCKS = 24
PAIRS = 11
BATCH = 4
MIB = 1024 * 1024


def swap_lanes(parts, low_bit, lane):
    count = len(parts)
    bit = 1
    while bit < count:
        shift = bit * low_bit
        clear = (lane & shift) == 0
        fresh = list(parts)
        for at in range(count):
            if at & bit == 0:
                low, high = parts[at], parts[at | bit]
                fresh[at] = jnp.where(clear, low, pltpu.roll(high, shift, 1))
                fresh[at | bit] = jnp.where(clear, pltpu.roll(low, TILE - shift, 1), high)
        parts = fresh
        bit *= 2
    return parts


def legendre_kernel(
    waves, spectral, legendre, derivative, factor, permute, out,
    spec_in, leg_in, der_in, sums, order, spec_sem, leg_sem, der_sem,
):
    slots = spectral.shape[0]
    lane = lax.broadcasted_iota(jnp.int32, (48, TILE), 1)
    half = TILE // 2
    cuts = NM // SPAN

    def copies(slot, cut):
        lanes = pl.ds(cut * SPAN, NM - cut * SPAN)
        return (
            pltpu.make_async_copy(
                legendre.at[slot, :, lanes], leg_in.at[slot, :, lanes], leg_sem.at[slot]
            ),
            pltpu.make_async_copy(
                derivative.at[slot, :, lanes], der_in.at[slot, :, lanes], der_sem.at[slot]
            ),
            pltpu.make_async_copy(
                spectral.at[slot, :, :, :, lanes], spec_in.at[slot, :, :, :, lanes], spec_sem.at[slot]
            ),
        )

    sizes = [jnp.int32(0)] * cuts
    for slot in range(slots):
        cut = waves[slot] // SPAN
        sizes = [size + (cut == at).astype(jnp.int32) for at, size in enumerate(sizes)]
    begins = [None] * cuts
    total = jnp.int32(0)
    for at in reversed(range(cuts)):
        begins[at] = total
        total = total + sizes[at]
    places = list(begins)
    for slot in range(slots):
        cut = waves[slot] // SPAN
        place = places[0]
        for at in range(1, cuts):
            place = jnp.where(cut == at, places[at], place)
        order[place] = slot
        places = [where + (cut == at).astype(jnp.int32) for at, where in enumerate(places)]

    for at in reversed(range(cuts)):

        def start(place, carry, at=at):
            for copy in copies(order[place], at):
                copy.start()
            return carry

        lax.fori_loop(begins[at], begins[at] + sizes[at], start, 0)

    for at in reversed(range(cuts)):
        first_lane = at * SPAN
        width = NM - first_lane
        end = begins[at] + sizes[at]

        def batch(step, carry, at=at, first_lane=first_lane, width=width, end=end):
            place = begins[at] + step * BATCH
            members = []
            for which in range(BATCH):
                slot = order[jnp.minimum(place + which, end - 1)]
                members.append(slot)

                @pl.when(place + which < end)
                def _(slot=slot):
                    for copy in copies(slot, at):
                        copy.wait()

            degree = lax.broadcasted_iota(jnp.int32, (8, width), 1) + first_lane
            scale = factor[:, first_lane:]
            results = []
            for slot in members:
                wave = waves[slot]
                live = degree >= wave
                odd = ((degree + wave) & 1) == 1
                keep_even = jnp.where(live & ~odd, 1.0, 0.0)
                keep_odd = jnp.where(live & odd, 1.0, 0.0)
                parts = [
                    spec_in[slot, field, side, :, first_lane:].astype(jnp.float32)
                    for field in range(2)
                    for side in range(2)
                ]
                rows = []
                for keep in (keep_even, keep_odd):
                    scaled = scale * keep
                    rows += [parts[0] * keep, parts[1] * keep]
                    rows += [part * scaled for part in parts]
                operand = jnp.concatenate(rows, axis=0).astype(jnp.bfloat16)
                both = jnp.concatenate(
                    [leg_in[slot, :, first_lane:], der_in[slot, :, first_lane:]], axis=0
                )
                results.append(
                    lax.dot_general(
                        operand, both, (((1,), (1,)), ((), ())), preferred_element_type=jnp.float32
                    )
                )
            for slot, result in zip(members, results):
                sums[slot] = result
            return carry

        lax.fori_loop(0, (sizes[at] + BATCH - 1) // BATCH, batch, 0)

    left = lane < half

    def finish(group, carry):
        parts = []
        for at in range(GROUP):
            slot = group * GROUP + at
            wave_float = waves[slot].astype(jnp.float32)
            even_sum, odd_sum = sums[slot, :48], sums[slot, 48:]
            north = even_sum + odd_sum
            south = even_sum - odd_sum
            value = jnp.where(left, north, pltpu.roll(south, half, 1))
            slope = jnp.where(left, pltpu.roll(north, half, 1), -south)
            parts.append(
                jnp.concatenate(
                    [
                        value[0:8],
                        -wave_float * value[40:48] - slope[16:24],
                        -wave_float * value[24:32] + slope[32:40],
                        value[8:16],
                        wave_float * value[32:40] - slope[24:32],
                        wave_float * value[16:24] + slope[40:48],
                    ],
                    axis=0,
                ).astype(jnp.bfloat16)
            )
        placed = jnp.dot(
            jnp.concatenate(parts, axis=0), permute[...], preferred_element_type=jnp.float32
        )
        parts = [placed[48 * at : 48 * at + 48] for at in range(GROUP)]
        for at, piece in enumerate(swap_lanes(parts, 1, lane)):
            out[at, group] = piece.astype(jnp.bfloat16)
        return carry

    lax.fori_loop(0, slots // GROUP, finish, 0)


def legendre_stage(spectral, legendre, derivative, own_waves, lat_order):
    slots = spectral.shape[0]
    groups = slots // GROUP
    degree = jnp.arange(NM, dtype=jnp.int32).astype(jnp.float32)
    factor = jnp.where(degree > 0, -float(NM) / jnp.maximum(degree * (degree + 1.0), 1.0), 0.0)
    factor = jnp.broadcast_to(factor[None, :], (8, NM))
    lane_row = lat_order.reshape(16, 8).T.reshape(TILE)
    permute = (jnp.arange(TILE, dtype=jnp.int32)[:, None] == lane_row[None, :]).astype(jnp.bfloat16)
    hbm = pl.BlockSpec(memory_space=pl.ANY)
    vmem = pl.BlockSpec(memory_space=pltpu.VMEM)
    return pl.pallas_call(
        legendre_kernel,
        in_specs=[pl.BlockSpec(memory_space=pltpu.SMEM), hbm, hbm, hbm, vmem, vmem],
        out_specs=vmem,
        scratch_shapes=[
            pltpu.VMEM((slots, 2, 2, 8, NM), jnp.bfloat16),
            pltpu.VMEM((slots, 64, NM), jnp.bfloat16),
            pltpu.VMEM((slots, 64, NM), jnp.bfloat16),
            pltpu.VMEM((slots, 96, TILE), jnp.float32),
            pltpu.SMEM((slots,), jnp.int32),
            pltpu.SemaphoreType.DMA((slots,)),
            pltpu.SemaphoreType.DMA((slots,)),
            pltpu.SemaphoreType.DMA((slots,)),
        ],
        out_shape=jax.ShapeDtypeStruct((16, groups, 48, TILE), jnp.bfloat16),
        compiler_params=pltpu.CompilerParams(vmem_limit_bytes=60 * MIB),
        cost_estimate=pl.CostEstimate(
            flops=slots * 96 * 128 * NM * 2, bytes_accessed=slots * 160 * NM * 2, transcendentals=0
        ),
    )(own_waves, spectral, legendre, derivative, factor, permute)


def turn_parts(product, length, inverse):
    turned = product - jnp.floor(product * inverse) * length
    turn = turned * inverse
    quarter = jnp.floor(turn * 4.0 + 0.5)
    angle = (turn - quarter * 0.25) * 6.283185307179586
    square = angle * angle
    sine = angle * (1.0 + square * (-1.0 / 6 + square * (1.0 / 120 + square * (-1.0 / 5040))))
    cosine = 1.0 + square * (
        -0.5 + square * (1.0 / 24 + square * (-1.0 / 720 + square * (1.0 / 40320)))
    )
    which = quarter.astype(jnp.int32)
    odd = (which & 1) == 1
    cos_sign = jnp.where(((which + 1) & 2) == 0, 1.0, -1.0)
    sin_sign = jnp.where((which & 2) == 0, 1.0, -1.0)
    return cos_sign * jnp.where(odd, sine, cosine), sin_sign * jnp.where(odd, cosine, sine)


def table_kernel(lengths, waves, table, base):
    length = lengths[pl.program_id(0)].astype(jnp.float32)
    spread = jnp.full((8, NM), length)
    inverse = (1.0 / spread)[:1]
    wave = waves[...]
    step = lax.broadcasted_iota(jnp.int32, (16, NM), 0).astype(jnp.float32)
    fine_cos, fine_sin = turn_parts(step * wave, length, inverse)
    coarse_cos, coarse_sin = turn_parts(step * wave * 16.0, length, inverse)
    for at in range(16):
        one_cos, one_sin = coarse_cos[at : at + 1], coarse_sin[at : at + 1]
        rows = slice(16 * at, 16 * at + 16)
        table[0, rows, :NM] = (one_cos * fine_cos - one_sin * fine_sin).astype(jnp.bfloat16)
        table[0, rows, NM:] = (-one_sin * fine_cos - one_cos * fine_sin).astype(jnp.bfloat16)
    block = lax.broadcasted_iota(jnp.int32, (BLOCKS, NM), 0).astype(jnp.float32)
    base_cos, base_sin = turn_parts(block * wave * float(SPAN), length, inverse)
    weight = jnp.where(wave == 0.0, 1.0, 2.0) * jnp.where(2.0 * wave < length, 1.0, 0.0)
    base[0, 0] = base_cos * weight
    base[0, 1] = base_sin * weight


def table_stage(lengths, wave_row):
    rows = lengths.shape[0]
    return pl.pallas_call(
        table_kernel,
        grid_spec=pltpu.PrefetchScalarGridSpec(
            num_scalar_prefetch=1,
            grid=(rows,),
            in_specs=[pl.BlockSpec((1, NM), lambda r, n: (0, 0))],
            out_specs=[
                pl.BlockSpec((1, SPAN, 2 * NM), lambda r, n: (r, 0, 0)),
                pl.BlockSpec((1, 2, BLOCKS, NM), lambda r, n: (r, 0, 0, 0)),
            ],
        ),
        out_shape=[
            jax.ShapeDtypeStruct((rows, SPAN, 2 * NM), jnp.bfloat16),
            jax.ShapeDtypeStruct((rows, 2, BLOCKS, NM), jnp.float32),
        ],
        compiler_params=pltpu.CompilerParams(vmem_limit_bytes=30 * MIB),
        cost_estimate=pl.CostEstimate(
            flops=rows * SPAN * NM * 10, bytes_accessed=rows * SPAN * NM * 5, transcendentals=0
        ),
    )(lengths, wave_row)


def fourier_kernel(lengths, slots, coeffs, table, base, out, highest, fields, turned, values, peak):
    row = pl.program_id(0)
    rows = pl.num_programs(0)
    lane = lax.broadcasted_iota(jnp.int32, (48, TILE), 1)

    @pl.when(row == 0)
    def _():
        peak[...] = jnp.zeros_like(peak)
        for group in range(5):
            for half in range(2):
                parts = [
                    coeffs[half * 8 + at, group].astype(jnp.float32) for at in range(8)
                ]
                tile = group * 2 + half
                for at, block in enumerate(swap_lanes(parts, 16, lane)):
                    fields[at, :, tile * TILE : tile * TILE + TILE] = block

    out[...] = jnp.zeros_like(out)
    length = lengths[row]
    pairs = (length + 2 * SPAN - 1) // (2 * SPAN)

    def turn(pair, carry):
        held = pl.ds(pl.multiple_of(pair * 48, 48), 48)
        for chunk in range(5):
            lanes = slice(chunk * 256, chunk * 256 + 256)
            shifted = slice(NM + chunk * 256, NM + chunk * 256 + 256)
            real = fields[row, 0:24, lanes]
            imag = fields[row, 24:48, lanes]
            turned_re, turned_im = [], []
            for side in range(2):
                cosine = base[0, 0, pl.ds(pair * 2 + side, 1), lanes]
                sine = base[0, 1, pl.ds(pair * 2 + side, 1), lanes]
                turned_re.append(real * cosine - imag * sine)
                turned_im.append(real * sine + imag * cosine)
            turned[held, lanes] = jnp.concatenate(turned_re, 0).astype(jnp.bfloat16)
            turned[held, shifted] = jnp.concatenate(turned_im, 0).astype(jnp.bfloat16)
        return carry

    lax.fori_loop(0, pairs, turn, 0)

    sizes = (2, 4, 6, 8, PAIRS)
    for at, size in enumerate(sizes):
        above = pairs > sizes[at - 1] if at else pairs > 0

        @pl.when(above & (pairs <= size))
        def _():
            values[: size * 48] = lax.dot_general(
                turned[: size * 48],
                table[0],
                (((1,), (1,)), ((), ())),
                preferred_element_type=jnp.float32,
            )

    column = lax.broadcasted_iota(jnp.int32, (24, TILE), 1)

    def store(pair, carry):
        best = peak[...]
        for block in range(2):
            for side in range(2):
                tile = pair * 4 + block * 2 + side
                piece = values[
                    pl.ds(pl.multiple_of(pair * 48 + block * 24, 8), 24),
                    side * TILE : side * TILE + TILE,
                ]
                piece = jnp.where(column + tile * TILE < length, piece, 0.0)
                rounded = piece.astype(jnp.bfloat16)
                slot = slots[tile]
                for field in range(3):
                    out[slot // 6, 0, slot % 6, field] = rounded[field * 8 : field * 8 + 8]
                best = jnp.maximum(best, rounded[:8].astype(jnp.float32))
        peak[...] = best
        return carry

    lax.fori_loop(0, pairs, store, 0)

    @pl.when(row == rows - 1)
    def _():
        highest[...] = jnp.full((8, TILE), jnp.max(peak[...]))


def fourier_stage(lengths, tile_slots, coeffs, table, base):
    rows = lengths.shape[0]
    return pl.pallas_call(
        fourier_kernel,
        grid_spec=pltpu.PrefetchScalarGridSpec(
            num_scalar_prefetch=2,
            grid=(rows,),
            in_specs=[
                pl.BlockSpec(coeffs.shape, lambda r, n, s: (0, 0, 0, 0)),
                pl.BlockSpec((1, SPAN, 2 * NM), lambda r, n, s: (r, 0, 0)),
                pl.BlockSpec((1, 2, BLOCKS, NM), lambda r, n, s: (r, 0, 0, 0)),
            ],
            out_specs=[
                pl.BlockSpec((8, 1, 6, 3, 8, TILE), lambda r, n, s: (0, r, 0, 0, 0, 0)),
                pl.BlockSpec((8, TILE), lambda r, n, s: (0, 0)),
            ],
            scratch_shapes=[
                pltpu.VMEM((rows, 48, NM), jnp.float32),
                pltpu.VMEM((PAIRS * 48, 2 * NM), jnp.bfloat16),
                pltpu.VMEM((PAIRS * 48, SPAN), jnp.float32),
                pltpu.VMEM((8, TILE), jnp.float32),
            ],
        ),
        out_shape=[
            jax.ShapeDtypeStruct((8, rows, 6, 3, 8, TILE), jnp.bfloat16),
            jax.ShapeDtypeStruct((8, TILE), jnp.float32),
        ],
        compiler_params=pltpu.CompilerParams(vmem_limit_bytes=40 * MIB),
        cost_estimate=pl.CostEstimate(
            flops=rows * 576 * 2 * NM * 256, bytes_accessed=rows * SPAN * NM * 5, transcendentals=0
        ),
    )(lengths, tile_slots, coeffs, table, base)


def shards(spectral, legendre, derivative, wave_order, lat_order, row_lengths, tile_map):
    wave_index = lax.axis_index("wave")
    slot_count = spectral.shape[0]
    own_waves = lax.dynamic_slice_in_dim(wave_order, wave_index * slot_count, slot_count)
    coeffs = legendre_stage(spectral, legendre, derivative, own_waves, lat_order)
    fourier = lax.all_to_all(coeffs, "wave", split_axis=0, concat_axis=0, tiled=True)

    row_ids = lax.dynamic_slice_in_dim(lat_order, wave_index * 8, 8)
    lengths = row_lengths[row_ids % 64]
    wave_row = wave_order.reshape(16, 5, GROUP).transpose(1, 0, 2).reshape(1, NM).astype(jnp.float32)
    table, base = table_stage(lengths, wave_row)
    tile_slots = jnp.zeros((48,), jnp.int32).at[tile_map].set(jnp.arange(48, dtype=jnp.int32))
    grid_part, highest = fourier_stage(lengths, tile_slots, fourier, table, base)
    received = lax.all_to_all(grid_part, "lev", split_axis=0, concat_axis=0, tiled=True)
    grid_values = received.transpose(1, 3, 0, 4, 2, 5).reshape(8, 3, 64, 768)
    highest = jnp.max(lax.all_gather(highest, "wave", axis=0), axis=0)
    hop = 1
    while hop < 8:
        pairs = [(at, at ^ hop) for at in range(8)]
        highest = jnp.maximum(highest, lax.ppermute(highest, "lev", pairs))
        hop *= 2
    return (grid_values, highest[0, 0])


def solution(mesh):
    placed = (
        P("wave", None, None, "lev", None),
        P("wave", None, None),
        P("wave", None, None),
        P(),
        P(),
        P(),
        P(),
    )
    return jax.shard_map(
        shards,
        mesh=mesh,
        in_specs=placed,
        out_specs=(P("wave", None, None, "lev"), P()),
        check_vma=False,
    )
```

profile of v0, /device:TPU:0, one launch (start us, length us, event | category | flops | bytes accessed | tf_op | source)
XLA Modules:
  0.0 108.6 jit_solution(8622027772916371326)
XLA Ops:
  0.6 0.0 copy-start
  0.7 0.7 reshape.37
  1.4 0.1 copy.10
  1.5 0.1 eq.18
  1.6 0.6 fusion.permute
  2.2 1.3 %dynamic_slice.7.waves = s32[80]{0:T(128)} dynamic-slice(s32[1280]{0:T(1024)} %param.10, s32[]{:T(128)S(6)} %select_n.31), dynamic_slice_sizes={80} | dynamic-slice | bytes 644 | tf_op jit(solution)/shard_map/dynamic_slice | solution.py:384
  3.5 0.6 broadcast_in_dim.17.factor
  4.1 0.0 copy-start.2
  4.1 0.0 copy-start.4
  4.1 0.0 copy-start.3
  4.1 18.7 %shard_map.86 = bf16[16,5,48,128]{3,2,1,0:T(8,128)(2,1)} custom-call(s32[80]{0:T(128)} %dynamic_slice.7.waves, bf16[80,2,2,8,1280]{4,3,2,1,0:T(8,128)(2,1)} %spectral.1, bf16[80,64,1280]{2,1,0:T(8,128)(2,1)} %legendre.1, bf16[80,64,1280]{2,1,0:T(8,128)(2,1)} %derivative.1, f32[8,1280]{1,0:T(8,128)} %broadcast_in_dim.17.factor, bf16[128,128]{1,0:T(8,128)(2,1)} %fusion.permute), custom_call_target="tpu_custom_call" | custom-call | flops 2516582400 | bytes 32768000 | tf_op jit(solution)/shard_map/pallas_call | solution.py:184
  22.8 7.7 %all-to-all-start = ((bf16[16,5,48,128]{3,2,1,0:T(8,128)(2,1)}), bf16[16,5,48,128]{3,2,1,0:T(8,128)(2,1)S(1)}, u32[]{:S(2)}, u32[]{:S(2)}) async-start(bf16[16,5,48,128]{3,2,1,0:T(8,128)(2,1)} %shard_map.86), calls=%async_computation | async-start | bytes 1966080 | tf_op jit(solution)/shard_map/all_to_all | solution.py:386
  30.5 0.0 copy-done.2
  30.5 0.1 convert_element_type.22
  30.6 0.1 convert_element_type.24.waves
  30.7 0.0 copy-done.4
  30.7 0.7 scatter_custom_fusion.slots
  31.5 0.0 copy-done.3
  31.5 0.1 compare_select_fusion.1
  31.6 0.0 copy-done
  31.6 0.6 gather_fusion
  32.2 7.1 %shard_map.87 = (bf16[8,256,2560]{2,1,0:T(8,128)(2,1)S(1)}, f32[8,2,24,1280]{3,2,1,0:T(8,128)S(1)}) custom-call(s32[8]{0:T(128)S(1)} %gather_fusion, f32[1,1280]{1,0:T(1,128)S(1)} %convert_element_type.24.waves), custom_call_target="tpu_custom_call" | custom-call | flops 26214400 | bytes 13107200 | tf_op jit(solution)/shard_map/pallas_call | solution.py:245
  39.3 0.0 copy-start.1
  39.3 4.0 %copy-done.1 = bf16[8,256,2560]{2,1,0:T(8,128)(2,1)} copy-done((bf16[8,256,2560]{2,1,0:T(8,128)(2,1)}, bf16[8,256,2560]{2,1,0:T(8,128)(2,1)S(1)}, u32[]{:S(2)}) %copy-start.1) | copy-done | bytes 10485784
  43.3 4.5 %all-to-all-done.coeffs = bf16[16,5,48,128]{3,2,1,0:T(8,128)(2,1)S(1)} async-done(((bf16[16,5,48,128]{3,2,1,0:T(8,128)(2,1)}), bf16[16,5,48,128]{3,2,1,0:T(8,128)(2,1)S(1)}, u32[]{:S(2)}, u32[]{:S(2)}) %all-to-all-start) | async-done | bytes 983072 | tf_op jit(solution)/shard_map/all_to_all | solution.py:386
  47.8 17.4 %shard_map.88 = (bf16[8,8,6,3,8,128]{5,4,3,2,1,0:T(8,128)(2,1)}, f32[8,128]{1,0:T(8,128)S(1)}) custom-call(s32[8]{0:T(128)S(1)} %gather_fusion, s32[48]{0:T(128)S(1)} %scatter_custom_fusion.slots, bf16[16,5,48,128]{3,2,1,0:T(8,128)(2,1)S(1)} %all-to-all-done.coeffs, bf16[8,256,2560]{2,1,0:T(8,128)(2,1)} %copy-done.1, ...), custom_call_target="tpu_custom_call" | custom-call | flops 3019898880 | bytes 13107200 | tf_op jit(solution)/shard_map/pallas_call | solution.py:349
  65.2 5.4 %all-to-all-start.1 = ((bf16[8,8,6,3,8,128]{5,4,3,2,1,0:T(8,128)(2,1)}), bf16[8,8,6,3,8,128]{5,4,3,2,1,0:T(8,128)(2,1)S(1)}, u32[]{:S(2)}, u32[]{:S(2)}) async-start(bf16[8,8,6,3,8,128]{5,4,3,2,1,0:T(8,128)(2,1)} %get-tuple-element.8), calls=%async_computation.1 | async-start | bytes 4718592 | tf_op jit(solution)/shard_map/all_to_all | solution.py:394
  70.6 19.4 %all-gather = f32[128,128]{1,0:T(8,128)S(1)} all-gather(f32[8,128]{1,0:T(8,128)S(1)} %get-tuple-element.9), channel_id=2, replica_groups=mesh['wave'=16,'lev'=8] {'wave'}, dimensions={0}, use_global_device_ids=true | all-gather | bytes 69632 | tf_op jit(solution)/shard_map/all_gather | solution.py:396
  90.1 2.1 %collective-permute-start = (f32[8,128]{1,0:T(8,128)S(1)}, f32[8,128]{1,0:T(8,128)S(1)}, u32[]{:S(2)}, u32[]{:S(2)}) collective-permute-start(f32[8,128]{1,0:T(8,128)S(1)} %bitcast_reduce_fusion), channel_id=1, source_target_pairs={{0,1},{1,0},{2,3},{3,2},{4,5},{5,4},{6,7},{7,6},{8,9},{9,8},{10,11... | collective-permute-start | bytes 12296 | tf_op jit(solution)/shard_map/ppermute | solution.py:400
  92.2 5.5 %collective-permute-done = f32[8,128]{1,0:T(8,128)S(1)} collective-permute-done((f32[8,128]{1,0:T(8,128)S(1)}, f32[8,128]{1,0:T(8,128)S(1)}, u32[]{:S(2)}, u32[]{:S(2)}) %collective-permute-start) | collective-permute-done | bytes 4128 | tf_op jit(solution)/shard_map/ppermute | solution.py:400
  97.7 2.7 %collective-permute-start.1 = (f32[8,128]{1,0:T(8,128)S(1)}, f32[8,128]{1,0:T(8,128)S(1)}, u32[]{:S(2)}, u32[]{:S(2)}) collective-permute-start(f32[8,128]{1,0:T(8,128)S(1)} %max.17), channel_id=1, source_target_pairs={{0,2},{1,3},{2,0},{3,1},{4,6},{5,7},{6,4},{7,5},{8,10},{9,11},{10,... | collective-permute-start | bytes 12296 | tf_op jit(solution)/shard_map/ppermute | solution.py:400
  100.4 2.4 %collective-permute-done.1 = f32[8,128]{1,0:T(8,128)S(1)} collective-permute-done((f32[8,128]{1,0:T(8,128)S(1)}, f32[8,128]{1,0:T(8,128)S(1)}, u32[]{:S(2)}, u32[]{:S(2)}) %collective-permute-start.1) | collective-permute-done | bytes 4128 | tf_op jit(solution)/shard_map/ppermute | solution.py:400
  102.8 1.5 %collective-permute-start.2 = (f32[8,128]{1,0:T(8,128)S(1)}, f32[8,128]{1,0:T(8,128)S(1)}, u32[]{:S(2)}, u32[]{:S(2)}) collective-permute-start(f32[8,128]{1,0:T(8,128)S(1)} %max.18), channel_id=1, source_target_pairs={{0,4},{1,5},{2,6},{3,7},{4,0},{5,1},{6,2},{7,3},{8,12},{9,13},{10,... | collective-permute-start | bytes 12296 | tf_op jit(solution)/shard_map/ppermute | solution.py:400
  104.3 2.1 %collective-permute-done.2 = f32[8,128]{1,0:T(8,128)S(1)} collective-permute-done((f32[8,128]{1,0:T(8,128)S(1)}, f32[8,128]{1,0:T(8,128)S(1)}, u32[]{:S(2)}, u32[]{:S(2)}) %collective-permute-start.2) | collective-permute-done | bytes 4128 | tf_op jit(solution)/shard_map/ppermute | solution.py:400
  106.4 0.5 slice.3
  106.9 0.0 all-to-all-done.1
  106.9 1.7 %copy_bitcast_fusion = bf16[8,3,64,768]{3,2,1,0:T(8,128)(2,1)} fusion(bf16[8,8,6,3,8,128]{5,4,3,2,1,0:T(8,128)(2,1)S(1)} %all-to-all-done.1), kind=kLoop, calls=%fused_computation.2 | loop fusion | bytes 4718592 | tf_op jit(solution)/shard_map/reshape | solution.py:395
  (10 shorter events, 0.1 us)
Async XLA Ops:
  0.6 31.0 %copy-start = (s32[64]{0:T(128)S(1)}, s32[64]{0:T(128)}, u32[]{:S(2)}) copy-start(s32[64]{0:T(128)} %param.12) | copy-start | bytes 772
  4.1 26.4 %copy-start.2 = (s32[1280]{0:T(1024)S(1)}, s32[1280]{0:T(1024)}, u32[]{:S(2)}) copy-start(s32[1280]{0:T(1024)} %param.10) | copy-start | bytes 15364
  4.1 26.6 %copy-start.4 = (s32[48]{0:T(128)S(1)}, s32[48]{0:T(128)}, u32[]{:S(2)}) copy-start(s32[48]{0:T(128)} %param.13) | copy-start | bytes 580
  4.1 27.4 %copy-start.3 = (s32[128]{0:T(128)S(1)}, s32[128]{0:T(128)}, u32[]{:S(2)}) copy-start(s32[128]{0:T(128)} %param.11) | copy-start | bytes 1540
  22.8 25.0 %all-to-all-start = ((bf16[16,5,48,128]{3,2,1,0:T(8,128)(2,1)}), bf16[16,5,48,128]{3,2,1,0:T(8,128)(2,1)S(1)}, u32[]{:S(2)}, u32[]{:S(2)}) async-start(bf16[16,5,48,128]{3,2,1,0:T(8,128)(2,1)} %shard_map.86), calls=%async_computation | async-start | bytes 1966080 | tf_op jit(solution)/shard_map/all_to_all | solution.py:386
  39.3 4.0 %copy-start.1 = (bf16[8,256,2560]{2,1,0:T(8,128)(2,1)}, bf16[8,256,2560]{2,1,0:T(8,128)(2,1)S(1)}, u32[]{:S(2)}) copy-start(bf16[8,256,2560]{2,1,0:T(8,128)(2,1)S(1)} %get-tuple-element.6.table) | copy-start | bytes 31457284
  65.2 41.8 %all-to-all-start.1 = ((bf16[8,8,6,3,8,128]{5,4,3,2,1,0:T(8,128)(2,1)}), bf16[8,8,6,3,8,128]{5,4,3,2,1,0:T(8,128)(2,1)S(1)}, u32[]{:S(2)}, u32[]{:S(2)}) async-start(bf16[8,8,6,3,8,128]{5,4,3,2,1,0:T(8,128)(2,1)} %get-tuple-element.8), calls=%async_computation.1 | async-start | bytes 4718592 | tf_op jit(solution)/shard_map/all_to_all | solution.py:394
  90.1 7.6 %collective-permute-start = (f32[8,128]{1,0:T(8,128)S(1)}, f32[8,128]{1,0:T(8,128)S(1)}, u32[]{:S(2)}, u32[]{:S(2)}) collective-permute-start(f32[8,128]{1,0:T(8,128)S(1)} %bitcast_reduce_fusion), channel_id=1, source_target_pairs={{0,1},{1,0},{2,3},{3,2},{4,5},{5,4},{6,7},{7,6},{8,9},{9,8},{10,11... | collective-permute-start | bytes 12296 | tf_op jit(solution)/shard_map/ppermute | solution.py:400
  97.7 5.1 %collective-permute-start.1 = (f32[8,128]{1,0:T(8,128)S(1)}, f32[8,128]{1,0:T(8,128)S(1)}, u32[]{:S(2)}, u32[]{:S(2)}) collective-permute-start(f32[8,128]{1,0:T(8,128)S(1)} %max.17), channel_id=1, source_target_pairs={{0,2},{1,3},{2,0},{3,1},{4,6},{5,7},{6,4},{7,5},{8,10},{9,11},{10,... | collective-permute-start | bytes 12296 | tf_op jit(solution)/shard_map/ppermute | solution.py:400
  102.8 3.6 %collective-permute-start.2 = (f32[8,128]{1,0:T(8,128)S(1)}, f32[8,128]{1,0:T(8,128)S(1)}, u32[]{:S(2)}, u32[]{:S(2)}) collective-permute-start(f32[8,128]{1,0:T(8,128)S(1)} %max.18), channel_id=1, source_target_pairs={{0,4},{1,5},{2,6},{3,7},{4,0},{5,1},{6,2},{7,3},{8,12},{9,13},{10,... | collective-permute-start | bytes 12296 | tf_op jit(solution)/shard_map/ppermute | solution.py:400
where the time goes:
time: 108 us; the launch traced here: 109 us
  Pallas kernels  43.2 us (40%)
  starting transfers between devices  19.4 us (18%)
  blocking collectives  19.4 us (18%)
  waiting for transfers between devices  14.6 us (14%)
  local copies, waits for them, and re-layouts  10.5 us (10%)
    all_gather x1, blocking collectives, shards(): highest = jnp.max(lax.all_gather(highest, 'wave', axis=0), axis=0)  19.4 us
    pallas_call x1, Pallas kernels, legendre_stage(): pl.pallas_call(legendre_kernel, in_specs=[pl.BlockSpec(memory_space=pltpu...  18.7 us
    pallas_call x1, Pallas kernels, fourier_stage(): pl.pallas_call(fourier_kernel, grid_spec=pltpu.PrefetchScalarGridSpec(num...  17.4 us
    ppermute x3, waiting for transfers between devices, shards(): highest = jnp.maximum(highest, lax.ppermute(highest, 'lev', pairs))  10.1 us
    all_to_all x1, starting transfers between devices, shards(): lax.all_to_all(coeffs, 'wave', split_axis=0, concat_axis=0, tiled=True)  7.71 us
    pallas_call x1, Pallas kernels, table_stage(): pl.pallas_call(table_kernel, grid_spec=pltpu.PrefetchScalarGridSpec(num_s...  7.07 us
    ppermute x3, starting transfers between devices, shards(): highest = jnp.maximum(highest, lax.ppermute(highest, 'lev', pairs))  6.23 us
    all_to_all x1, starting transfers between devices, shards(): lax.all_to_all(grid_part, 'lev', split_axis=0, concat_axis=0, tiled=True)  5.42 us
  transfers between devices with their start and end apart: 5, of which 4 were waited for; matrix products, arithmetic and copies ran while one was open for 2% of the time, Pallas kernels for 7%

commit v1 on v0

--- a/solution.py
+++ b/solution.py
@@ -35,8 +35,8 @@
 
 
 def legendre_kernel(
-    waves, spectral, legendre, derivative, factor, permute, out,
-    spec_in, leg_in, der_in, sums, order, spec_sem, leg_sem, der_sem,
+    all_waves, lat_row, spectral, legendre, derivative, out,
+    spec_in, leg_in, der_in, sums, factor, permute, waves, order, spec_sem, leg_sem, der_sem,
 ):
     slots = spectral.shape[0]
     lane = lax.broadcasted_iota(jnp.int32, (48, TILE), 1)
@@ -57,8 +57,10 @@
             ),
         )
 
+    own = lax.axis_index("wave") * slots
     sizes = [jnp.int32(0)] * cuts
     for slot in range(slots):
+        waves[slot] = all_waves[own + slot]
         cut = waves[slot] // SPAN
         sizes = [size + (cut == at).astype(jnp.int32) for at, size in enumerate(sizes)]
     begins = [None] * cuts
@@ -83,6 +85,14 @@
             return carry
 
         lax.fori_loop(begins[at], begins[at] + sizes[at], start, 0)
+
+    number = lax.broadcasted_iota(jnp.int32, (8, NM), 1).astype(jnp.float32)
+    factor[...] = jnp.where(number > 0, -float(NM) / jnp.maximum(number * (number + 1.0), 1.0), 0.0)
+    down = lax.broadcasted_iota(jnp.int32, (TILE, TILE), 0)
+    across = lax.broadcasted_iota(jnp.int32, (TILE, TILE), 1)
+    at_row = jnp.where(down == lat_row[...], 1.0, 0.0).astype(jnp.bfloat16)
+    at_lane = jnp.where(down == (across % 16) * 8 + across // 16, 1.0, 0.0).astype(jnp.bfloat16)
+    permute[...] = jnp.dot(at_row, at_lane, preferred_element_type=jnp.float32).astype(jnp.bfloat16)
 
     for at in reversed(range(cuts)):
         first_lane = at * SPAN
@@ -163,33 +173,32 @@
         placed = jnp.dot(
             jnp.concatenate(parts, axis=0), permute[...], preferred_element_type=jnp.float32
         )
+        placed = placed.astype(jnp.bfloat16)
         parts = [placed[48 * at : 48 * at + 48] for at in range(GROUP)]
         for at, piece in enumerate(swap_lanes(parts, 1, lane)):
-            out[at, group] = piece.astype(jnp.bfloat16)
+            out[at, group] = piece
         return carry
 
     lax.fori_loop(0, slots // GROUP, finish, 0)
 
 
-def legendre_stage(spectral, legendre, derivative, own_waves, lat_order):
+def legendre_stage(spectral, legendre, derivative, wave_order, lat_order):
     slots = spectral.shape[0]
     groups = slots // GROUP
-    degree = jnp.arange(NM, dtype=jnp.int32).astype(jnp.float32)
-    factor = jnp.where(degree > 0, -float(NM) / jnp.maximum(degree * (degree + 1.0), 1.0), 0.0)
-    factor = jnp.broadcast_to(factor[None, :], (8, NM))
-    lane_row = lat_order.reshape(16, 8).T.reshape(TILE)
-    permute = (jnp.arange(TILE, dtype=jnp.int32)[:, None] == lane_row[None, :]).astype(jnp.bfloat16)
     hbm = pl.BlockSpec(memory_space=pl.ANY)
     vmem = pl.BlockSpec(memory_space=pltpu.VMEM)
     return pl.pallas_call(
         legendre_kernel,
-        in_specs=[pl.BlockSpec(memory_space=pltpu.SMEM), hbm, hbm, hbm, vmem, vmem],
+        in_specs=[pl.BlockSpec(memory_space=pltpu.SMEM), vmem, hbm, hbm, hbm],
         out_specs=vmem,
         scratch_shapes=[
             pltpu.VMEM((slots, 2, 2, 8, NM), jnp.bfloat16),
             pltpu.VMEM((slots, 64, NM), jnp.bfloat16),
             pltpu.VMEM((slots, 64, NM), jnp.bfloat16),
             pltpu.VMEM((slots, 96, TILE), jnp.float32),
+            pltpu.VMEM((8, NM), jnp.float32),
+            pltpu.VMEM((TILE, TILE), jnp.bfloat16),
+            pltpu.SMEM((slots,), jnp.int32),
             pltpu.SMEM((slots,), jnp.int32),
             pltpu.SemaphoreType.DMA((slots,)),
             pltpu.SemaphoreType.DMA((slots,)),
@@ -200,7 +209,7 @@
         cost_estimate=pl.CostEstimate(
             flops=slots * 96 * 128 * NM * 2, bytes_accessed=slots * 160 * NM * 2, transcendentals=0
         ),
-    )(own_waves, spectral, legendre, derivative, factor, permute)
+    )(wave_order, lat_order.reshape(1, TILE), spectral, legendre, derivative)
 
 
 def turn_parts(product, length, inverse):
@@ -221,152 +230,146 @@
 
 
 def table_kernel(lengths, waves, table, base):
-    length = lengths[pl.program_id(0)].astype(jnp.float32)
-    spread = jnp.full((8, NM), length)
-    inverse = (1.0 / spread)[:1]
     wave = waves[...]
     step = lax.broadcasted_iota(jnp.int32, (16, NM), 0).astype(jnp.float32)
-    fine_cos, fine_sin = turn_parts(step * wave, length, inverse)
-    coarse_cos, coarse_sin = turn_parts(step * wave * 16.0, length, inverse)
-    for at in range(16):
-        one_cos, one_sin = coarse_cos[at : at + 1], coarse_sin[at : at + 1]
-        rows = slice(16 * at, 16 * at + 16)
-        table[0, rows, :NM] = (one_cos * fine_cos - one_sin * fine_sin).astype(jnp.bfloat16)
-        table[0, rows, NM:] = (-one_sin * fine_cos - one_cos * fine_sin).astype(jnp.bfloat16)
     block = lax.broadcasted_iota(jnp.int32, (BLOCKS, NM), 0).astype(jnp.float32)
-    base_cos, base_sin = turn_parts(block * wave * float(SPAN), length, inverse)
-    weight = jnp.where(wave == 0.0, 1.0, 2.0) * jnp.where(2.0 * wave < length, 1.0, 0.0)
-    base[0, 0] = base_cos * weight
-    base[0, 1] = base_sin * weight
+
+    def one_row(row, carry):
+        length = lengths[row].astype(jnp.float32)
+        inverse = (1.0 / jnp.full((8, NM), length))[:1]
+        fine_cos, fine_sin = turn_parts(step * wave, length, inverse)
+        coarse_cos, coarse_sin = turn_parts(step * wave * 16.0, length, inverse)
+        for at in range(16):
+            one_cos, one_sin = coarse_cos[at : at + 1], coarse_sin[at : at + 1]
+            span = slice(16 * at, 16 * at + 16)
+            table[row, span, :NM] = (one_cos * fine_cos - one_sin * fine_sin).astype(jnp.bfloat16)
+            table[row, span, NM:] = (-one_sin * fine_cos - one_cos * fine_sin).astype(jnp.bfloat16)
+        base_cos, base_sin = turn_parts(block * wave * float(SPAN), length, inverse)
+        weight = jnp.where(wave == 0.0, 1.0, 2.0) * jnp.where(2.0 * wave < length, 1.0, 0.0)
+        base[row, 0] = base_cos * weight
+        base[row, 1] = base_sin * weight
+        return carry
+
+    lax.fori_loop(0, table.shape[0], one_row, 0)
 
 
 def table_stage(lengths, wave_row):
     rows = lengths.shape[0]
+    vmem = pl.BlockSpec(memory_space=pltpu.VMEM)
     return pl.pallas_call(
         table_kernel,
-        grid_spec=pltpu.PrefetchScalarGridSpec(
-            num_scalar_prefetch=1,
-            grid=(rows,),
-            in_specs=[pl.BlockSpec((1, NM), lambda r, n: (0, 0))],
-            out_specs=[
-                pl.BlockSpec((1, SPAN, 2 * NM), lambda r, n: (r, 0, 0)),
-                pl.BlockSpec((1, 2, BLOCKS, NM), lambda r, n: (r, 0, 0, 0)),
-            ],
-        ),
+        in_specs=[pl.BlockSpec(memory_space=pltpu.SMEM), vmem],
+        out_specs=[vmem, vmem],
         out_shape=[
             jax.ShapeDtypeStruct((rows, SPAN, 2 * NM), jnp.bfloat16),
             jax.ShapeDtypeStruct((rows, 2, BLOCKS, NM), jnp.float32),
         ],
         compiler_params=pltpu.CompilerParams(vmem_limit_bytes=30 * MIB),
         cost_estimate=pl.CostEstimate(
-            flops=rows * SPAN * NM * 10, bytes_accessed=rows * SPAN * NM * 5, transcendentals=0
+            flops=rows * SPAN * NM * 40, bytes_accessed=rows * SPAN * NM * 5, transcendentals=0
         ),
     )(lengths, wave_row)
 
 
-def fourier_kernel(lengths, slots, coeffs, table, base, out, highest, fields, turned, values, peak):
-    row = pl.program_id(0)
-    rows = pl.num_programs(0)
+def fourier_kernel(
+    lengths, slots, coeffs, table, base, out, highest,
+    fields, turned, values, peak, staged, out_sem,
+):
+    rows = table.shape[0]
     lane = lax.broadcasted_iota(jnp.int32, (48, TILE), 1)
-
-    @pl.when(row == 0)
-    def _():
-        peak[...] = jnp.zeros_like(peak)
-        for group in range(5):
-            for half in range(2):
-                parts = [
-                    coeffs[half * 8 + at, group].astype(jnp.float32) for at in range(8)
-                ]
-                tile = group * 2 + half
-                for at, block in enumerate(swap_lanes(parts, 16, lane)):
-                    fields[at, :, tile * TILE : tile * TILE + TILE] = block
-
-    out[...] = jnp.zeros_like(out)
-    length = lengths[row]
-    pairs = (length + 2 * SPAN - 1) // (2 * SPAN)
-
-    def turn(pair, carry):
-        held = pl.ds(pl.multiple_of(pair * 48, 48), 48)
-        for chunk in range(5):
-            lanes = slice(chunk * 256, chunk * 256 + 256)
-            shifted = slice(NM + chunk * 256, NM + chunk * 256 + 256)
-            real = fields[row, 0:24, lanes]
-            imag = fields[row, 24:48, lanes]
-            turned_re, turned_im = [], []
-            for side in range(2):
-                cosine = base[0, 0, pl.ds(pair * 2 + side, 1), lanes]
-                sine = base[0, 1, pl.ds(pair * 2 + side, 1), lanes]
-                turned_re.append(real * cosine - imag * sine)
-                turned_im.append(real * sine + imag * cosine)
-            turned[held, lanes] = jnp.concatenate(turned_re, 0).astype(jnp.bfloat16)
-            turned[held, shifted] = jnp.concatenate(turned_im, 0).astype(jnp.bfloat16)
+    column = lax.broadcasted_iota(jnp.int32, (24, TILE), 1)
+
+    def result(row):
+        return pltpu.make_async_copy(staged.at[:, row], out.at[:, row], out_sem.at[row])
+
+    peak[...] = jnp.zeros_like(peak)
+    for group in range(5):
+        for half in range(2):
+            parts = [coeffs[half * 8 + at, group] for at in range(8)]
+            tile = group * 2 + half
+            for at, block in enumerate(swap_lanes(parts, 16, lane)):
+                fields[at, :, tile * TILE : tile * TILE + TILE] = block.astype(jnp.float32)
+
+    def one_row(row, carry):
+        length = lengths[row]
+        pairs = (length + 2 * SPAN - 1) // (2 * SPAN)
+        staged[:, row] = jnp.zeros((8, 6, 3, 8, TILE), jnp.bfloat16)
+        sizes = (2, 4, 6, 8, PAIRS)
+        for at, size in enumerate(sizes):
+            above = pairs > sizes[at - 1] if at else pairs > 0
+
+            @pl.when(above & (pairs <= size))
+            def _(size=size):
+                for chunk in range(5):
+                    lanes = slice(chunk * 256, chunk * 256 + 256)
+                    shifted = slice(NM + chunk * 256, NM + chunk * 256 + 256)
+                    real = fields[row, 0:24, lanes]
+                    imag = fields[row, 24:48, lanes]
+                    for pair in range(size):
+                        held = slice(pair * 48, pair * 48 + 48)
+                        turned_re, turned_im = [], []
+                        for side in range(2):
+                            which = pair * 2 + side
+                            cosine = base[row, 0, which : which + 1, lanes]
+                            sine = base[row, 1, which : which + 1, lanes]
+                            turned_re.append(real * cosine - imag * sine)
+                            turned_im.append(real * sine + imag * cosine)
+                        turned[held, lanes] = jnp.concatenate(turned_re, 0).astype(jnp.bfloat16)
+                        turned[held, shifted] = jnp.concatenate(turned_im, 0).astype(jnp.bfloat16)
+                values[: size * 48] = lax.dot_general(
+                    turned[: size * 48],
+                    table[row],
+                    (((1,), (1,)), ((), ())),
+                    preferred_element_type=jnp.float32,
+                )
+
+        def store(pair, inner):
+            best = peak[...]
+            for block in range(2):
+                for side in range(2):
+                    tile = pair * 4 + block * 2 + side
+                    piece = values[
+                        pl.ds(pl.multiple_of(pair * 48 + block * 24, 8), 24),
+                        side * TILE : side * TILE + TILE,
+                    ]
+                    piece = jnp.where(column + tile * TILE < length, piece, 0.0)
+                    rounded = piece.astype(jnp.bfloat16)
+                    at_slot = slots[tile]
+                    for field in range(3):
+                        staged[at_slot // 6, row, at_slot % 6, field] = rounded[
+                            field * 8 : field * 8 + 8
+                        ]
+                    best = jnp.maximum(best, rounded[:8].astype(jnp.float32))
+            peak[...] = best
+            return inner
+
+        lax.fori_loop(0, pairs, store, 0)
+        result(row).start()
         return carry
 
-    lax.fori_loop(0, pairs, turn, 0)
-
-    sizes = (2, 4, 6, 8, PAIRS)
-    for at, size in enumerate(sizes):
-        above = pairs > sizes[at - 1] if at else pairs > 0
-
-        @pl.when(above & (pairs <= size))
-        def _():
-            values[: size * 48] = lax.dot_general(
-                turned[: size * 48],
-                table[0],
-                (((1,), (1,)), ((), ())),
-                preferred_element_type=jnp.float32,
-            )
-
-    column = lax.broadcasted_iota(jnp.int32, (24, TILE), 1)
-
-    def store(pair, carry):
-        best = peak[...]
-        for block in range(2):
-            for side in range(2):
-                tile = pair * 4 + block * 2 + side
-                piece = values[
-                    pl.ds(pl.multiple_of(pair * 48 + block * 24, 8), 24),
-                    side * TILE : side * TILE + TILE,
-                ]
-                piece = jnp.where(column + tile * TILE < length, piece, 0.0)
-                rounded = piece.astype(jnp.bfloat16)
-                slot = slots[tile]
-                for field in range(3):
-                    out[slot // 6, 0, slot % 6, field] = rounded[field * 8 : field * 8 + 8]
-                best = jnp.maximum(best, rounded[:8].astype(jnp.float32))
-        peak[...] = best
-        return carry
-
-    lax.fori_loop(0, pairs, store, 0)
-
-    @pl.when(row == rows - 1)
-    def _():
-        highest[...] = jnp.full((8, TILE), jnp.max(peak[...]))
+    lax.fori_loop(0, rows, one_row, 0)
+    highest[...] = jnp.full((8, TILE), jnp.max(peak[...]))
+    for row in range(rows):
+        result(row).wait()
 
 
 def fourier_stage(lengths, tile_slots, coeffs, table, base):
     rows = lengths.shape[0]
+    scalar = pl.BlockSpec(memory_space=pltpu.SMEM)
+    vmem = pl.BlockSpec(memory_space=pltpu.VMEM)
+    hbm = pl.BlockSpec(memory_space=pl.ANY)
     return pl.pallas_call(
         fourier_kernel,
-        grid_spec=pltpu.PrefetchScalarGridSpec(
-            num_scalar_prefetch=2,
-            grid=(rows,),
-            in_specs=[
-                pl.BlockSpec(coeffs.shape, lambda r, n, s: (0, 0, 0, 0)),
-                pl.BlockSpec((1, SPAN, 2 * NM), lambda r, n, s: (r, 0, 0)),
-                pl.BlockSpec((1, 2, BLOCKS, NM), lambda r, n, s: (r, 0, 0, 0)),
-            ],
-            out_specs=[
-                pl.BlockSpec((8, 1, 6, 3, 8, TILE), lambda r, n, s: (0, r, 0, 0, 0, 0)),
-                pl.BlockSpec((8, TILE), lambda r, n, s: (0, 0)),
-            ],
-            scratch_shapes=[
-                pltpu.VMEM((rows, 48, NM), jnp.float32),
-                pltpu.VMEM((PAIRS * 48, 2 * NM), jnp.bfloat16),
-                pltpu.VMEM((PAIRS * 48, SPAN), jnp.float32),
-                pltpu.VMEM((8, TILE), jnp.float32),
-            ],
-        ),
+        in_specs=[scalar, scalar, vmem, vmem, vmem],
+        out_specs=[hbm, vmem],
+        scratch_shapes=[
+            pltpu.VMEM((rows, 48, NM), jnp.float32),
+            pltpu.VMEM((PAIRS * 48, 2 * NM), jnp.bfloat16),
+            pltpu.VMEM((PAIRS * 48, SPAN), jnp.float32),
+            pltpu.VMEM((8, TILE), jnp.float32),
+            pltpu.VMEM((8, rows, 6, 3, 8, TILE), jnp.bfloat16),
+            pltpu.SemaphoreType.DMA((rows,)),
+        ],
         out_shape=[
             jax.ShapeDtypeStruct((8, rows, 6, 3, 8, TILE), jnp.bfloat16),
             jax.ShapeDtypeStruct((8, TILE), jnp.float32),
@@ -380,9 +383,7 @@
 
 def shards(spectral, legendre, derivative, wave_order, lat_order, row_lengths, tile_map):
     wave_index = lax.axis_index("wave")
-    slot_count = spectral.shape[0]
-    own_waves = lax.dynamic_slice_in_dim(wave_order, wave_index * slot_count, slot_count)
-    coeffs = legendre_stage(spectral, legendre, derivative, own_waves, lat_order)
+    coeffs = legendre_stage(spectral, legendre, derivative, wave_order, lat_order)
     fourier = lax.all_to_all(coeffs, "wave", split_axis=0, concat_axis=0, tiled=True)
 
     row_ids = lax.dynamic_slice_in_dim(lat_order, wave_index * 8, 8)

time: 108 us -> 103 us (0.954)
  Pallas kernels: 43.2 us -> 40.2 us
  local copies, waits for them, and re-layouts: 10.5 us -> 7.74 us
  blocking collectives: 19.4 us -> 20.9 us
    pallas_call x2, Pallas kernels: 24.5 us -> 21.1 us  [the longest x1 14.1 us: fourier_stage(): pl.pallas_call(fourier_kernel, in_specs=[scalar, scalar, vmem, vmem, vmem...]
    all_gather x1, blocking collectives: 19.4 us -> 20.9 us  [shards(): highest = jnp.max(lax.all_gather(highest, 'wave', axis=0), axis=0)]
    dynamic_slice x1 -> x0, local copies, waits for them, and re-layouts: 1.28 us -> none  [shards(): lax.dynamic_slice_in_dim(wave_order, wave_index * slot_count, slot_count)]
where the time goes in v1:
time: 103 us; the launch traced here: 104 us
  Pallas kernels  40.2 us (39%)
  blocking collectives  20.9 us (20%)
  starting transfers between devices  19.1 us (19%)
  waiting for transfers between devices  14.9 us (14%)
  local copies, waits for them, and re-layouts  7.74 us (8%)
    all_gather x1, blocking collectives, shards(): highest = jnp.max(lax.all_gather(highest, 'wave', axis=0), axis=0)  20.9 us
    pallas_call x1, Pallas kernels, legendre_stage(): pl.pallas_call(legendre_kernel, in_specs=[pl.BlockSpec(memory_space=pltpu...  19.1 us
    pallas_call x1, Pallas kernels, fourier_stage(): pl.pallas_call(fourier_kernel, in_specs=[scalar, scalar, vmem, vmem, vmem...  14.1 us
    ppermute x3, waiting for transfers between devices, shards(): highest = jnp.maximum(highest, lax.ppermute(highest, 'lev', pairs))  10.3 us
    all_to_all x1, starting transfers between devices, shards(): lax.all_to_all(coeffs, 'wave', split_axis=0, concat_axis=0, tiled=True)  7.38 us
    pallas_call x1, Pallas kernels, table_stage(): pl.pallas_call(table_kernel, in_specs=[pl.BlockSpec(memory_space=pltpu.SM...  7.03 us
    ppermute x3, starting transfers between devices, shards(): highest = jnp.maximum(highest, lax.ppermute(highest, 'lev', pairs))  6.27 us
    all_to_all x1, starting transfers between devices, shards(): lax.all_to_all(grid_part, 'lev', split_axis=0, concat_axis=0, tiled=True)  5.44 us
  transfers between devices with their start and end apart: 5, of which 4 were waited for; matrix products, arithmetic and copies ran while one was open for 2% of the time, Pallas kernels for 7%

profile of v1, /device:TPU:0, one launch (start us, length us, event | category | flops | bytes accessed | tf_op | source)
XLA Modules:
  0.0 103.7 jit_solution(9571749249713426560)
XLA Ops:
  0.6 0.0 copy-start
  0.6 0.0 copy-start.2
  0.7 0.0 copy-start.4
  0.7 0.0 copy-start.3
  0.7 19.1 %shard_map.86 = bf16[16,5,48,128]{3,2,1,0:T(8,128)(2,1)} custom-call(s32[1280]{0:T(1024)} %all_waves.1, s32[1,128]{1,0:T(1,128)} %bitcast.12, bf16[80,2,2,8,1280]{4,3,2,1,0:T(8,128)(2,1)} %spectral.1, bf16[80,64,1280]{2,1,0:T(8,128)(2,1)} %legendre.1, bf16[80,64,1280]{2,1,0:T(8,128)(2,1)} %derivative.1), custom_call_target="tpu_custom_call" | custom-call | flops 2516582400 | bytes 32768000 | tf_op jit(solution)/shard_map/pallas_call | solution.py:190
  19.8 7.4 %all-to-all-start = ((bf16[16,5,48,128]{3,2,1,0:T(8,128)(2,1)}), bf16[16,5,48,128]{3,2,1,0:T(8,128)(2,1)S(1)}, u32[]{:S(2)}, u32[]{:S(2)}) async-start(bf16[16,5,48,128]{3,2,1,0:T(8,128)(2,1)} %shard_map.86), calls=%async_computation | async-start | bytes 1966080 | tf_op jit(solution)/shard_map/all_to_all | solution.py:387
  27.2 0.0 copy-done.2
  27.2 0.1 convert_element_type.10
  27.3 0.1 convert_element_type.12.waves
  27.4 0.0 copy-done.4
  27.5 0.7 scatter_custom_fusion.slots
  28.2 0.0 copy-done.3
  28.2 0.1 compare_select_fusion.1
  28.3 0.0 copy-done
  28.3 0.6 gather_fusion
  28.9 7.0 %shard_map.87 = (bf16[8,256,2560]{2,1,0:T(8,128)(2,1)S(1)}, f32[8,2,24,1280]{3,2,1,0:T(8,128)S(1)}) custom-call(s32[8]{0:T(128)S(1)} %gather_fusion, f32[1,1280]{1,0:T(1,128)S(1)} %convert_element_type.12.waves), custom_call_target="tpu_custom_call" | custom-call | flops 104857600 | bytes 13107200 | tf_op jit(solution)/shard_map/pallas_call | solution.py:259
  36.0 0.0 copy-start.1
  36.0 4.0 %copy-done.1 = bf16[8,256,2560]{2,1,0:T(8,128)(2,1)} copy-done((bf16[8,256,2560]{2,1,0:T(8,128)(2,1)}, bf16[8,256,2560]{2,1,0:T(8,128)(2,1)S(1)}, u32[]{:S(2)}) %copy-start.1) | copy-done | bytes 10485784
  40.0 4.5 %all-to-all-done.coeffs = bf16[16,5,48,128]{3,2,1,0:T(8,128)(2,1)S(1)} async-done(((bf16[16,5,48,128]{3,2,1,0:T(8,128)(2,1)}), bf16[16,5,48,128]{3,2,1,0:T(8,128)(2,1)S(1)}, u32[]{:S(2)}, u32[]{:S(2)}) %all-to-all-start) | async-done | bytes 983072 | tf_op jit(solution)/shard_map/all_to_all | solution.py:387
  44.5 14.1 %shard_map.88 = (bf16[8,8,6,3,8,128]{5,4,3,2,1,0:T(8,128)(2,1)}, f32[8,128]{1,0:T(8,128)S(1)}) custom-call(s32[8]{0:T(128)S(1)} %gather_fusion, s32[48]{0:T(128)S(1)} %scatter_custom_fusion.slots, bf16[16,5,48,128]{3,2,1,0:T(8,128)(2,1)S(1)} %all-to-all-done.coeffs, bf16[8,256,2560]{2,1,0:T(8,128)(2,1)} %copy-done.1, ...), custom_call_target="tpu_custom_call" | custom-call | flops 3019898880 | bytes 13107200 | tf_op jit(solution)/shard_map/pallas_call | solution.py:361
  58.6 5.4 %all-to-all-start.1 = ((bf16[8,8,6,3,8,128]{5,4,3,2,1,0:T(8,128)(2,1)}), bf16[8,8,6,3,8,128]{5,4,3,2,1,0:T(8,128)(2,1)S(1)}, u32[]{:S(2)}, u32[]{:S(2)}) async-start(bf16[8,8,6,3,8,128]{5,4,3,2,1,0:T(8,128)(2,1)} %get-tuple-element.8), calls=%async_computation.1 | async-start | bytes 4718592 | tf_op jit(solution)/shard_map/all_to_all | solution.py:395
  64.0 20.9 %all-gather = f32[128,128]{1,0:T(8,128)S(1)} all-gather(f32[8,128]{1,0:T(8,128)S(1)} %get-tuple-element.9), channel_id=2, replica_groups=mesh['wave'=16,'lev'=8] {'wave'}, dimensions={0}, use_global_device_ids=true | all-gather | bytes 69632 | tf_op jit(solution)/shard_map/all_gather | solution.py:397
  84.9 1.8 %collective-permute-start = (f32[8,128]{1,0:T(8,128)S(1)}, f32[8,128]{1,0:T(8,128)S(1)}, u32[]{:S(2)}, u32[]{:S(2)}) collective-permute-start(f32[8,128]{1,0:T(8,128)S(1)} %bitcast_reduce_fusion), channel_id=1, source_target_pairs={{0,1},{1,0},{2,3},{3,2},{4,5},{5,4},{6,7},{7,6},{8,9},{9,8},{10,11... | collective-permute-start | bytes 12296 | tf_op jit(solution)/shard_map/ppermute | solution.py:401
  86.7 6.1 %collective-permute-done = f32[8,128]{1,0:T(8,128)S(1)} collective-permute-done((f32[8,128]{1,0:T(8,128)S(1)}, f32[8,128]{1,0:T(8,128)S(1)}, u32[]{:S(2)}, u32[]{:S(2)}) %collective-permute-start) | collective-permute-done | bytes 4128 | tf_op jit(solution)/shard_map/ppermute | solution.py:401
  92.8 2.7 %collective-permute-start.1 = (f32[8,128]{1,0:T(8,128)S(1)}, f32[8,128]{1,0:T(8,128)S(1)}, u32[]{:S(2)}, u32[]{:S(2)}) collective-permute-start(f32[8,128]{1,0:T(8,128)S(1)} %max.9), channel_id=1, source_target_pairs={{0,2},{1,3},{2,0},{3,1},{4,6},{5,7},{6,4},{7,5},{8,10},{9,11},{10,... | collective-permute-start | bytes 12296 | tf_op jit(solution)/shard_map/ppermute | solution.py:401
  95.5 2.4 %collective-permute-done.1 = f32[8,128]{1,0:T(8,128)S(1)} collective-permute-done((f32[8,128]{1,0:T(8,128)S(1)}, f32[8,128]{1,0:T(8,128)S(1)}, u32[]{:S(2)}, u32[]{:S(2)}) %collective-permute-start.1) | collective-permute-done | bytes 4128 | tf_op jit(solution)/shard_map/ppermute | solution.py:401
  97.9 1.8 %collective-permute-start.2 = (f32[8,128]{1,0:T(8,128)S(1)}, f32[8,128]{1,0:T(8,128)S(1)}, u32[]{:S(2)}, u32[]{:S(2)}) collective-permute-start(f32[8,128]{1,0:T(8,128)S(1)} %max.10), channel_id=1, source_target_pairs={{0,4},{1,5},{2,6},{3,7},{4,0},{5,1},{6,2},{7,3},{8,12},{9,13},{10,... | collective-permute-start | bytes 12296 | tf_op jit(solution)/shard_map/ppermute | solution.py:401
  99.7 1.8 %collective-permute-done.2 = f32[8,128]{1,0:T(8,128)S(1)} collective-permute-done((f32[8,128]{1,0:T(8,128)S(1)}, f32[8,128]{1,0:T(8,128)S(1)}, u32[]{:S(2)}, u32[]{:S(2)}) %collective-permute-start.2) | collective-permute-done | bytes 4128 | tf_op jit(solution)/shard_map/ppermute | solution.py:401
  101.5 0.5 slice.3
  102.0 0.0 all-to-all-done.1
  102.0 1.7 %copy_bitcast_fusion = bf16[8,3,64,768]{3,2,1,0:T(8,128)(2,1)} fusion(bf16[8,8,6,3,8,128]{5,4,3,2,1,0:T(8,128)(2,1)S(1)} %all-to-all-done.1), kind=kLoop, calls=%fused_computation.2 | loop fusion | bytes 4718592 | tf_op jit(solution)/shard_map/reshape | solution.py:396
  (9 shorter events, 0.1 us)
Async XLA Ops:
  0.6 27.7 %copy-start = (s32[64]{0:T(128)S(1)}, s32[64]{0:T(128)}, u32[]{:S(2)}) copy-start(s32[64]{0:T(128)} %param.12) | copy-start | bytes 772
  0.6 26.6 %copy-start.2 = (s32[1280]{0:T(1024)S(1)}, s32[1280]{0:T(1024)}, u32[]{:S(2)}) copy-start(s32[1280]{0:T(1024)} %all_waves.1) | copy-start | bytes 15364
  0.7 26.8 %copy-start.4 = (s32[48]{0:T(128)S(1)}, s32[48]{0:T(128)}, u32[]{:S(2)}) copy-start(s32[48]{0:T(128)} %param.13) | copy-start | bytes 580
  0.7 27.5 %copy-start.3 = (s32[128]{0:T(128)S(1)}, s32[128]{0:T(128)}, u32[]{:S(2)}) copy-start(s32[128]{0:T(128)} %param.11) | copy-start | bytes 1540
  19.8 24.7 %all-to-all-start = ((bf16[16,5,48,128]{3,2,1,0:T(8,128)(2,1)}), bf16[16,5,48,128]{3,2,1,0:T(8,128)(2,1)S(1)}, u32[]{:S(2)}, u32[]{:S(2)}) async-start(bf16[16,5,48,128]{3,2,1,0:T(8,128)(2,1)} %shard_map.86), calls=%async_computation | async-start | bytes 1966080 | tf_op jit(solution)/shard_map/all_to_all | solution.py:387
  36.0 4.0 %copy-start.1 = (bf16[8,256,2560]{2,1,0:T(8,128)(2,1)}, bf16[8,256,2560]{2,1,0:T(8,128)(2,1)S(1)}, u32[]{:S(2)}) copy-start(bf16[8,256,2560]{2,1,0:T(8,128)(2,1)S(1)} %get-tuple-element.6.table) | copy-start | bytes 31457284
  58.6 43.5 %all-to-all-start.1 = ((bf16[8,8,6,3,8,128]{5,4,3,2,1,0:T(8,128)(2,1)}), bf16[8,8,6,3,8,128]{5,4,3,2,1,0:T(8,128)(2,1)S(1)}, u32[]{:S(2)}, u32[]{:S(2)}) async-start(bf16[8,8,6,3,8,128]{5,4,3,2,1,0:T(8,128)(2,1)} %get-tuple-element.8), calls=%async_computation.1 | async-start | bytes 4718592 | tf_op jit(solution)/shard_map/all_to_all | solution.py:395
  84.9 7.9 %collective-permute-start = (f32[8,128]{1,0:T(8,128)S(1)}, f32[8,128]{1,0:T(8,128)S(1)}, u32[]{:S(2)}, u32[]{:S(2)}) collective-permute-start(f32[8,128]{1,0:T(8,128)S(1)} %bitcast_reduce_fusion), channel_id=1, source_target_pairs={{0,1},{1,0},{2,3},{3,2},{4,5},{5,4},{6,7},{7,6},{8,9},{9,8},{10,11... | collective-permute-start | bytes 12296 | tf_op jit(solution)/shard_map/ppermute | solution.py:401
  92.8 5.1 %collective-permute-start.1 = (f32[8,128]{1,0:T(8,128)S(1)}, f32[8,128]{1,0:T(8,128)S(1)}, u32[]{:S(2)}, u32[]{:S(2)}) collective-permute-start(f32[8,128]{1,0:T(8,128)S(1)} %max.9), channel_id=1, source_target_pairs={{0,2},{1,3},{2,0},{3,1},{4,6},{5,7},{6,4},{7,5},{8,10},{9,11},{10,... | collective-permute-start | bytes 12296 | tf_op jit(solution)/shard_map/ppermute | solution.py:401
  97.9 3.6 %collective-permute-start.2 = (f32[8,128]{1,0:T(8,128)S(1)}, f32[8,128]{1,0:T(8,128)S(1)}, u32[]{:S(2)}, u32[]{:S(2)}) collective-permute-start(f32[8,128]{1,0:T(8,128)S(1)} %max.10), channel_id=1, source_target_pairs={{0,4},{1,5},{2,6},{3,7},{4,0},{5,1},{6,2},{7,3},{8,12},{9,13},{10,... | collective-permute-start | bytes 12296 | tf_op jit(solution)/shard_map/ppermute | solution.py:401

commit v2 on v1

--- a/solution.py
+++ b/solution.py
@@ -41,7 +41,7 @@
     slots = spectral.shape[0]
     lane = lax.broadcasted_iota(jnp.int32, (48, TILE), 1)
     half = TILE // 2
-    cuts = NM // SPAN
+    cuts = 4
 
     def copies(slot, cut):
         lanes = pl.ds(cut * SPAN, NM - cut * SPAN)
@@ -58,24 +58,22 @@
         )
 
     own = lax.axis_index("wave") * slots
-    sizes = [jnp.int32(0)] * cuts
+    tally = jnp.int32(0)
     for slot in range(slots):
-        waves[slot] = all_waves[own + slot]
-        cut = waves[slot] // SPAN
-        sizes = [size + (cut == at).astype(jnp.int32) for at, size in enumerate(sizes)]
+        wave = all_waves[own + slot]
+        waves[slot] = wave
+        tally = tally + lax.shift_left(jnp.int32(1), jnp.minimum(wave >> 8, cuts - 1) << 3)
+    sizes = [(tally >> (8 * at)) & 127 for at in range(cuts)]
     begins = [None] * cuts
     total = jnp.int32(0)
     for at in reversed(range(cuts)):
         begins[at] = total
         total = total + sizes[at]
-    places = list(begins)
+    places = sum(begins[at] << (8 * at) for at in range(cuts))
     for slot in range(slots):
-        cut = waves[slot] // SPAN
-        place = places[0]
-        for at in range(1, cuts):
-            place = jnp.where(cut == at, places[at], place)
-        order[place] = slot
-        places = [where + (cut == at).astype(jnp.int32) for at, where in enumerate(places)]
+        shift = jnp.minimum(waves[slot] >> 8, cuts - 1) << 3
+        order[lax.shift_right_logical(places, shift) & 127] = slot
+        places = places + lax.shift_left(jnp.int32(1), shift)
 
     for at in reversed(range(cuts)):
 
@@ -143,7 +141,7 @@
                 sums[slot] = result
             return carry
 
-        lax.fori_loop(0, (sizes[at] + BATCH - 1) // BATCH, batch, 0)
+        lax.fori_loop(0, (sizes[at] + BATCH - 1) >> 2, batch, 0)
 
     left = lane < half
 
@@ -292,7 +290,7 @@
 
     def one_row(row, carry):
         length = lengths[row]
-        pairs = (length + 2 * SPAN - 1) // (2 * SPAN)
+        pairs = (length + 2 * SPAN - 1) >> 9
         staged[:, row] = jnp.zeros((8, 6, 3, 8, TILE), jnp.bfloat16)
         sizes = (2, 4, 6, 8, PAIRS)
         for at, size in enumerate(sizes):
@@ -334,11 +332,9 @@
                     ]
                     piece = jnp.where(column + tile * TILE < length, piece, 0.0)
                     rounded = piece.astype(jnp.bfloat16)
-                    at_slot = slots[tile]
+                    owner, place = slots[0, tile], slots[1, tile]
                     for field in range(3):
-                        staged[at_slot // 6, row, at_slot % 6, field] = rounded[
-                            field * 8 : field * 8 + 8
-                        ]
+                        staged[owner, row, place, field] = rounded[field * 8 : field * 8 + 8]
                     best = jnp.maximum(best, rounded[:8].astype(jnp.float32))
             peak[...] = best
             return inner
@@ -391,6 +387,7 @@
     wave_row = wave_order.reshape(16, 5, GROUP).transpose(1, 0, 2).reshape(1, NM).astype(jnp.float32)
     table, base = table_stage(lengths, wave_row)
     tile_slots = jnp.zeros((48,), jnp.int32).at[tile_map].set(jnp.arange(48, dtype=jnp.int32))
+    tile_slots = jnp.stack([tile_slots // 6, tile_slots % 6])
     grid_part, highest = fourier_stage(lengths, tile_slots, fourier, table, base)
     received = lax.all_to_all(grid_part, "lev", split_axis=0, concat_axis=0, tiled=True)
     grid_values = received.transpose(1, 3, 0, 4, 2, 5).reshape(8, 3, 64, 768)

time: 103 us -> 101 us (0.981)
  waiting for transfers between devices: 14.9 us -> 12.8 us
  Pallas kernels: 40.2 us -> 38.6 us
    ppermute x3, waiting for transfers between devices: 10.3 us -> 8.31 us  [shards(): highest = jnp.maximum(highest, lax.ppermute(highest, 'lev', pairs))]
    pallas_call x1, Pallas kernels: 19.1 us -> 18 us  [legendre_stage(): pl.pallas_call(legendre_kernel, in_specs=[pl.BlockSpec(memory_space=pltpu...]
where the time goes in v2:
time: 101 us
  Pallas kernels  38.6 us (38%)
  blocking collectives  21.7 us (21%)
  starting transfers between devices  19.1 us (19%)
  waiting for transfers between devices  12.8 us (13%)
  local copies, waits for them, and re-layouts  7.73 us (8%)
    all_gather x1, blocking collectives, shards(): highest = jnp.max(lax.all_gather(highest, 'wave', axis=0), axis=0)  21.7 us
    pallas_call x1, Pallas kernels, legendre_stage(): pl.pallas_call(legendre_kernel, in_specs=[pl.BlockSpec(memory_space=pltpu...  18 us
    pallas_call x1, Pallas kernels, fourier_stage(): pl.pallas_call(fourier_kernel, in_specs=[scalar, scalar, vmem, vmem, vmem...  13.6 us
    ppermute x3, waiting for transfers between devices, shards(): highest = jnp.maximum(highest, lax.ppermute(highest, 'lev', pairs))  8.31 us
    all_to_all x1, starting transfers between devices, shards(): lax.all_to_all(coeffs, 'wave', split_axis=0, concat_axis=0, tiled=True)  7.34 us
    pallas_call x1, Pallas kernels, table_stage(): pl.pallas_call(table_kernel, in_specs=[pl.BlockSpec(memory_space=pltpu.SM...  7.03 us
    ppermute x3, starting transfers between devices, shards(): highest = jnp.maximum(highest, lax.ppermute(highest, 'lev', pairs))  6.29 us
    all_to_all x1, starting transfers between devices, shards(): lax.all_to_all(grid_part, 'lev', split_axis=0, concat_axis=0, tiled=True)  5.44 us
  transfers between devices with their start and end apart: 5, of which 4 were waited for; matrix products, arithmetic and copies ran while one was open for 2% of the time, Pallas kernels for 7%

profile of v2, /device:TPU:0, one launch (start us, length us, event | category | flops | bytes accessed | tf_op | source)
XLA Modules:
  0.0 100.9 jit_solution(3059846591944633019)
XLA Ops:
  0.6 0.0 copy-start
  0.6 0.0 copy-start.2
  0.7 0.0 copy-start.4
  0.7 0.0 copy-start.3
  0.7 18.0 %shard_map.86 = bf16[16,5,48,128]{3,2,1,0:T(8,128)(2,1)} custom-call(s32[1280]{0:T(1024)} %all_waves.1, s32[1,128]{1,0:T(1,128)} %bitcast.16, bf16[80,2,2,8,1280]{4,3,2,1,0:T(8,128)(2,1)} %spectral.1, bf16[80,64,1280]{2,1,0:T(8,128)(2,1)} %legendre.1, bf16[80,64,1280]{2,1,0:T(8,128)(2,1)} %derivative.1), custom_call_target="tpu_custom_call" | custom-call | flops 2516582400 | bytes 32768000 | tf_op jit(solution)/shard_map/pallas_call | solution.py:188
  18.7 7.3 %all-to-all-start = ((bf16[16,5,48,128]{3,2,1,0:T(8,128)(2,1)}), bf16[16,5,48,128]{3,2,1,0:T(8,128)(2,1)S(1)}, u32[]{:S(2)}, u32[]{:S(2)}) async-start(bf16[16,5,48,128]{3,2,1,0:T(8,128)(2,1)} %shard_map.86), calls=%async_computation | async-start | bytes 1966080 | tf_op jit(solution)/shard_map/all_to_all | solution.py:383
  26.1 0.0 copy-done.2
  26.1 0.1 convert_element_type.10
  26.2 0.1 convert_element_type.12.waves
  26.3 0.0 copy-done.4
  26.3 0.7 scatter_custom_fusion
  27.1 0.0 copy-done.3
  27.1 0.1 compare_select_fusion.1
  27.2 0.0 copy-done
  27.2 0.6 gather_fusion
  27.8 7.0 %shard_map.87 = (bf16[8,256,2560]{2,1,0:T(8,128)(2,1)S(1)}, f32[8,2,24,1280]{3,2,1,0:T(8,128)S(1)}) custom-call(s32[8]{0:T(128)S(1)} %gather_fusion, f32[1,1280]{1,0:T(1,128)S(1)} %convert_element_type.12.waves), custom_call_target="tpu_custom_call" | custom-call | flops 104857600 | bytes 13107200 | tf_op jit(solution)/shard_map/pallas_call | solution.py:257
  34.8 0.0 copy-start.1
  34.9 4.0 %copy-done.1 = bf16[8,256,2560]{2,1,0:T(8,128)(2,1)} copy-done((bf16[8,256,2560]{2,1,0:T(8,128)(2,1)}, bf16[8,256,2560]{2,1,0:T(8,128)(2,1)S(1)}, u32[]{:S(2)}) %copy-start.1) | copy-done | bytes 10485784
  38.8 4.5 %all-to-all-done.coeffs = bf16[16,5,48,128]{3,2,1,0:T(8,128)(2,1)S(1)} async-done(((bf16[16,5,48,128]{3,2,1,0:T(8,128)(2,1)}), bf16[16,5,48,128]{3,2,1,0:T(8,128)(2,1)S(1)}, u32[]{:S(2)}, u32[]{:S(2)}) %all-to-all-start) | async-done | bytes 983072 | tf_op jit(solution)/shard_map/all_to_all | solution.py:383
  43.3 13.6 %shard_map.88 = (bf16[8,8,6,3,8,128]{5,4,3,2,1,0:T(8,128)(2,1)}, f32[8,128]{1,0:T(8,128)S(1)}) custom-call(s32[8]{0:T(128)S(1)} %gather_fusion, s32[2,48]{1,0:T(2,128)S(1)} %pad_add_fusion.slots, bf16[16,5,48,128]{3,2,1,0:T(8,128)(2,1)S(1)} %all-to-all-done.coeffs, bf16[8,256,2560]{2,1,0:T(8,128)(2,1)} %copy-done.1, f32[8,2,24,1280]{3,2,1,0:T(8,128)S(1)} %get-tuple-element.7.base), custom_call_target="tpu_custom_call" | custom-call | flops 3019898880 | bytes 13107200 | tf_op jit(solution)/shard_map/pallas_call | solution.py:357
  56.9 5.4 %all-to-all-start.1 = ((bf16[8,8,6,3,8,128]{5,4,3,2,1,0:T(8,128)(2,1)}), bf16[8,8,6,3,8,128]{5,4,3,2,1,0:T(8,128)(2,1)S(1)}, u32[]{:S(2)}, u32[]{:S(2)}) async-start(bf16[8,8,6,3,8,128]{5,4,3,2,1,0:T(8,128)(2,1)} %get-tuple-element.8), calls=%async_computation.1 | async-start | bytes 4718592 | tf_op jit(solution)/shard_map/all_to_all | solution.py:392
  62.4 21.7 %all-gather = f32[128,128]{1,0:T(8,128)S(1)} all-gather(f32[8,128]{1,0:T(8,128)S(1)} %get-tuple-element.9), channel_id=2, replica_groups=mesh['wave'=16,'lev'=8] {'wave'}, dimensions={0}, use_global_device_ids=true | all-gather | bytes 69632 | tf_op jit(solution)/shard_map/all_gather | solution.py:394
  84.0 2.2 %collective-permute-start = (f32[8,128]{1,0:T(8,128)S(1)}, f32[8,128]{1,0:T(8,128)S(1)}, u32[]{:S(2)}, u32[]{:S(2)}) collective-permute-start(f32[8,128]{1,0:T(8,128)S(1)} %bitcast_reduce_fusion), channel_id=1, source_target_pairs={{0,1},{1,0},{2,3},{3,2},{4,5},{5,4},{6,7},{7,6},{8,9},{9,8},{10,11... | collective-permute-start | bytes 12296 | tf_op jit(solution)/shard_map/ppermute | solution.py:398
  86.2 3.7 %collective-permute-done = f32[8,128]{1,0:T(8,128)S(1)} collective-permute-done((f32[8,128]{1,0:T(8,128)S(1)}, f32[8,128]{1,0:T(8,128)S(1)}, u32[]{:S(2)}, u32[]{:S(2)}) %collective-permute-start) | collective-permute-done | bytes 4128 | tf_op jit(solution)/shard_map/ppermute | solution.py:398
  89.9 2.7 %collective-permute-start.1 = (f32[8,128]{1,0:T(8,128)S(1)}, f32[8,128]{1,0:T(8,128)S(1)}, u32[]{:S(2)}, u32[]{:S(2)}) collective-permute-start(f32[8,128]{1,0:T(8,128)S(1)} %max.9), channel_id=1, source_target_pairs={{0,2},{1,3},{2,0},{3,1},{4,6},{5,7},{6,4},{7,5},{8,10},{9,11},{10,... | collective-permute-start | bytes 12296 | tf_op jit(solution)/shard_map/ppermute | solution.py:398
  92.6 2.4 %collective-permute-done.1 = f32[8,128]{1,0:T(8,128)S(1)} collective-permute-done((f32[8,128]{1,0:T(8,128)S(1)}, f32[8,128]{1,0:T(8,128)S(1)}, u32[]{:S(2)}, u32[]{:S(2)}) %collective-permute-start.1) | collective-permute-done | bytes 4128 | tf_op jit(solution)/shard_map/ppermute | solution.py:398
  95.0 1.5 %collective-permute-start.2 = (f32[8,128]{1,0:T(8,128)S(1)}, f32[8,128]{1,0:T(8,128)S(1)}, u32[]{:S(2)}, u32[]{:S(2)}) collective-permute-start(f32[8,128]{1,0:T(8,128)S(1)} %max.10), channel_id=1, source_target_pairs={{0,4},{1,5},{2,6},{3,7},{4,0},{5,1},{6,2},{7,3},{8,12},{9,13},{10,... | collective-permute-start | bytes 12296 | tf_op jit(solution)/shard_map/ppermute | solution.py:398
  96.5 2.1 %collective-permute-done.2 = f32[8,128]{1,0:T(8,128)S(1)} collective-permute-done((f32[8,128]{1,0:T(8,128)S(1)}, f32[8,128]{1,0:T(8,128)S(1)}, u32[]{:S(2)}, u32[]{:S(2)}) %collective-permute-start.2) | collective-permute-done | bytes 4128 | tf_op jit(solution)/shard_map/ppermute | solution.py:398
  98.7 0.5 slice.3
  99.2 0.0 all-to-all-done.1
  99.2 1.7 %copy_bitcast_fusion = bf16[8,3,64,768]{3,2,1,0:T(8,128)(2,1)} fusion(bf16[8,8,6,3,8,128]{5,4,3,2,1,0:T(8,128)(2,1)S(1)} %all-to-all-done.1), kind=kLoop, calls=%fused_computation.2 | loop fusion | bytes 4718592 | tf_op jit(solution)/shard_map/reshape | solution.py:393
  (11 shorter events, 0.1 us)
Async XLA Ops:
  0.6 26.5 %copy-start = (s32[64]{0:T(128)S(1)}, s32[64]{0:T(128)}, u32[]{:S(2)}) copy-start(s32[64]{0:T(128)} %param.12) | copy-start | bytes 772
  0.6 25.4 %copy-start.2 = (s32[1280]{0:T(1024)S(1)}, s32[1280]{0:T(1024)}, u32[]{:S(2)}) copy-start(s32[1280]{0:T(1024)} %all_waves.1) | copy-start | bytes 15364
  0.7 25.6 %copy-start.4 = (s32[48]{0:T(128)S(1)}, s32[48]{0:T(128)}, u32[]{:S(2)}) copy-start(s32[48]{0:T(128)} %param.13) | copy-start | bytes 580
  0.7 26.4 %copy-start.3 = (s32[128]{0:T(128)S(1)}, s32[128]{0:T(128)}, u32[]{:S(2)}) copy-start(s32[128]{0:T(128)} %param.11) | copy-start | bytes 1540
  18.7 24.6 %all-to-all-start = ((bf16[16,5,48,128]{3,2,1,0:T(8,128)(2,1)}), bf16[16,5,48,128]{3,2,1,0:T(8,128)(2,1)S(1)}, u32[]{:S(2)}, u32[]{:S(2)}) async-start(bf16[16,5,48,128]{3,2,1,0:T(8,128)(2,1)} %shard_map.86), calls=%async_computation | async-start | bytes 1966080 | tf_op jit(solution)/shard_map/all_to_all | solution.py:383
  34.8 4.0 %copy-start.1 = (bf16[8,256,2560]{2,1,0:T(8,128)(2,1)}, bf16[8,256,2560]{2,1,0:T(8,128)(2,1)S(1)}, u32[]{:S(2)}) copy-start(bf16[8,256,2560]{2,1,0:T(8,128)(2,1)S(1)} %get-tuple-element.6.table) | copy-start | bytes 31457284
  56.9 42.3 %all-to-all-start.1 = ((bf16[8,8,6,3,8,128]{5,4,3,2,1,0:T(8,128)(2,1)}), bf16[8,8,6,3,8,128]{5,4,3,2,1,0:T(8,128)(2,1)S(1)}, u32[]{:S(2)}, u32[]{:S(2)}) async-start(bf16[8,8,6,3,8,128]{5,4,3,2,1,0:T(8,128)(2,1)} %get-tuple-element.8), calls=%async_computation.1 | async-start | bytes 4718592 | tf_op jit(solution)/shard_map/all_to_all | solution.py:392
  84.0 5.9 %collective-permute-start = (f32[8,128]{1,0:T(8,128)S(1)}, f32[8,128]{1,0:T(8,128)S(1)}, u32[]{:S(2)}, u32[]{:S(2)}) collective-permute-start(f32[8,128]{1,0:T(8,128)S(1)} %bitcast_reduce_fusion), channel_id=1, source_target_pairs={{0,1},{1,0},{2,3},{3,2},{4,5},{5,4},{6,7},{7,6},{8,9},{9,8},{10,11... | collective-permute-start | bytes 12296 | tf_op jit(solution)/shard_map/ppermute | solution.py:398
  89.9 5.1 %collective-permute-start.1 = (f32[8,128]{1,0:T(8,128)S(1)}, f32[8,128]{1,0:T(8,128)S(1)}, u32[]{:S(2)}, u32[]{:S(2)}) collective-permute-start(f32[8,128]{1,0:T(8,128)S(1)} %max.9), channel_id=1, source_target_pairs={{0,2},{1,3},{2,0},{3,1},{4,6},{5,7},{6,4},{7,5},{8,10},{9,11},{10,... | collective-permute-start | bytes 12296 | tf_op jit(solution)/shard_map/ppermute | solution.py:398
  95.0 3.6 %collective-permute-start.2 = (f32[8,128]{1,0:T(8,128)S(1)}, f32[8,128]{1,0:T(8,128)S(1)}, u32[]{:S(2)}, u32[]{:S(2)}) collective-permute-start(f32[8,128]{1,0:T(8,128)S(1)} %max.10), channel_id=1, source_target_pairs={{0,4},{1,5},{2,6},{3,7},{4,0},{5,1},{6,2},{7,3},{8,12},{9,13},{10,... | collective-permute-start | bytes 12296 | tf_op jit(solution)/shard_map/ppermute | solution.py:398

commit v3 on v2

--- a/solution.py
+++ b/solution.py
@@ -392,11 +392,9 @@
     received = lax.all_to_all(grid_part, "lev", split_axis=0, concat_axis=0, tiled=True)
     grid_values = received.transpose(1, 3, 0, 4, 2, 5).reshape(8, 3, 64, 768)
     highest = jnp.max(lax.all_gather(highest, "wave", axis=0), axis=0)
-    hop = 1
-    while hop < 8:
+    for hop in (4, 2, 1):
         pairs = [(at, at ^ hop) for at in range(8)]
         highest = jnp.maximum(highest, lax.ppermute(highest, "lev", pairs))
-        hop *= 2
     return (grid_values, highest[0, 0])
 
 

time: 101 us -> 101 us (level)
  starting transfers between devices: 19.1 us -> 17.9 us
  Pallas kernels: 38.6 us -> 39.8 us
where the time goes in v3:
time: 101 us; the launch traced here: 100 us
  Pallas kernels  39.8 us (39%)
  blocking collectives  21.2 us (21%)
  starting transfers between devices  17.9 us (18%)
  waiting for transfers between devices  12.6 us (12%)
  local copies, waits for them, and re-layouts  7.73 us (8%)
    all_gather x1, blocking collectives, shards(): highest = jnp.max(lax.all_gather(highest, 'wave', axis=0), axis=0)  21.2 us
    pallas_call x1, Pallas kernels, legendre_stage(): pl.pallas_call(legendre_kernel, in_specs=[pl.BlockSpec(memory_space=pltpu...  18.3 us
    pallas_call x1, Pallas kernels, fourier_stage(): pl.pallas_call(fourier_kernel, in_specs=[scalar, scalar, vmem, vmem, vmem...  14.5 us
    ppermute x3, waiting for transfers between devices, shards(): highest = jnp.maximum(highest, lax.ppermute(highest, 'lev', pairs))  8.14 us
    pallas_call x1, Pallas kernels, table_stage(): pl.pallas_call(table_kernel, in_specs=[pl.BlockSpec(memory_space=pltpu.SM...  7.03 us
    all_to_all x1, starting transfers between devices, shards(): lax.all_to_all(coeffs, 'wave', split_axis=0, concat_axis=0, tiled=True)  6.48 us
    ppermute x3, starting transfers between devices, shards(): highest = jnp.maximum(highest, lax.ppermute(highest, 'lev', pairs))  5.94 us
    all_to_all x1, starting transfers between devices, shards(): lax.all_to_all(grid_part, 'lev', split_axis=0, concat_axis=0, tiled=True)  5.44 us
  transfers between devices with their start and end apart: 5, of which 4 were waited for; matrix products, arithmetic and copies ran while one was open for 2% of the time, Pallas kernels for 7%

profile of v3, /device:TPU:0, one launch (start us, length us, event | category | flops | bytes accessed | tf_op | source)
XLA Modules:
  0.0 100.3 jit_solution(11702660633170251908)
XLA Ops:
  0.6 0.0 copy-start
  0.6 0.0 copy-start.2
  0.7 0.0 copy-start.4
  0.7 0.0 copy-start.3
  0.7 18.3 %shard_map.86 = bf16[16,5,48,128]{3,2,1,0:T(8,128)(2,1)} custom-call(s32[1280]{0:T(1024)} %all_waves.1, s32[1,128]{1,0:T(1,128)} %bitcast.16, bf16[80,2,2,8,1280]{4,3,2,1,0:T(8,128)(2,1)} %spectral.1, bf16[80,64,1280]{2,1,0:T(8,128)(2,1)} %legendre.1, bf16[80,64,1280]{2,1,0:T(8,128)(2,1)} %derivative.1), custom_call_target="tpu_custom_call" | custom-call | flops 2516582400 | bytes 32768000 | tf_op jit(solution)/shard_map/pallas_call | solution.py:188
  19.0 6.5 %all-to-all-start = ((bf16[16,5,48,128]{3,2,1,0:T(8,128)(2,1)}), bf16[16,5,48,128]{3,2,1,0:T(8,128)(2,1)S(1)}, u32[]{:S(2)}, u32[]{:S(2)}) async-start(bf16[16,5,48,128]{3,2,1,0:T(8,128)(2,1)} %shard_map.86), calls=%async_computation | async-start | bytes 1966080 | tf_op jit(solution)/shard_map/all_to_all | solution.py:383
  25.5 0.0 copy-done.2
  25.6 0.1 convert_element_type.10
  25.7 0.1 convert_element_type.12.waves
  25.7 0.0 copy-done.4
  25.8 0.7 scatter_custom_fusion
  26.5 0.0 copy-done.3
  26.5 0.1 compare_select_fusion.1
  26.6 0.0 copy-done
  26.6 0.6 gather_fusion
  27.3 7.0 %shard_map.87 = (bf16[8,256,2560]{2,1,0:T(8,128)(2,1)S(1)}, f32[8,2,24,1280]{3,2,1,0:T(8,128)S(1)}) custom-call(s32[8]{0:T(128)S(1)} %gather_fusion, f32[1,1280]{1,0:T(1,128)S(1)} %convert_element_type.12.waves), custom_call_target="tpu_custom_call" | custom-call | flops 104857600 | bytes 13107200 | tf_op jit(solution)/shard_map/pallas_call | solution.py:257
  34.3 0.0 copy-start.1
  34.3 4.0 %copy-done.1 = bf16[8,256,2560]{2,1,0:T(8,128)(2,1)} copy-done((bf16[8,256,2560]{2,1,0:T(8,128)(2,1)}, bf16[8,256,2560]{2,1,0:T(8,128)(2,1)S(1)}, u32[]{:S(2)}) %copy-start.1) | copy-done | bytes 10485784
  38.3 4.5 %all-to-all-done.coeffs = bf16[16,5,48,128]{3,2,1,0:T(8,128)(2,1)S(1)} async-done(((bf16[16,5,48,128]{3,2,1,0:T(8,128)(2,1)}), bf16[16,5,48,128]{3,2,1,0:T(8,128)(2,1)S(1)}, u32[]{:S(2)}, u32[]{:S(2)}) %all-to-all-start) | async-done | bytes 983072 | tf_op jit(solution)/shard_map/all_to_all | solution.py:383
  42.8 14.5 %shard_map.88 = (bf16[8,8,6,3,8,128]{5,4,3,2,1,0:T(8,128)(2,1)}, f32[8,128]{1,0:T(8,128)S(1)}) custom-call(s32[8]{0:T(128)S(1)} %gather_fusion, s32[2,48]{1,0:T(2,128)S(1)} %pad_add_fusion.slots, bf16[16,5,48,128]{3,2,1,0:T(8,128)(2,1)S(1)} %all-to-all-done.coeffs, bf16[8,256,2560]{2,1,0:T(8,128)(2,1)} %copy-done.1, f32[8,2,24,1280]{3,2,1,0:T(8,128)S(1)} %get-tuple-element.7.base), custom_call_target="tpu_custom_call" | custom-call | flops 3019898880 | bytes 13107200 | tf_op jit(solution)/shard_map/pallas_call | solution.py:357
  57.3 5.4 %all-to-all-start.1 = ((bf16[8,8,6,3,8,128]{5,4,3,2,1,0:T(8,128)(2,1)}), bf16[8,8,6,3,8,128]{5,4,3,2,1,0:T(8,128)(2,1)S(1)}, u32[]{:S(2)}, u32[]{:S(2)}) async-start(bf16[8,8,6,3,8,128]{5,4,3,2,1,0:T(8,128)(2,1)} %get-tuple-element.8), calls=%async_computation.1 | async-start | bytes 4718592 | tf_op jit(solution)/shard_map/all_to_all | solution.py:392
  62.7 21.2 %all-gather = f32[128,128]{1,0:T(8,128)S(1)} all-gather(f32[8,128]{1,0:T(8,128)S(1)} %get-tuple-element.9), channel_id=2, replica_groups=mesh['wave'=16,'lev'=8] {'wave'}, dimensions={0}, use_global_device_ids=true | all-gather | bytes 69632 | tf_op jit(solution)/shard_map/all_gather | solution.py:394
  84.0 1.5 %collective-permute-start = (f32[8,128]{1,0:T(8,128)S(1)}, f32[8,128]{1,0:T(8,128)S(1)}, u32[]{:S(2)}, u32[]{:S(2)}) collective-permute-start(f32[8,128]{1,0:T(8,128)S(1)} %bitcast_reduce_fusion), channel_id=1, source_target_pairs={{0,4},{1,5},{2,6},{3,7},{4,0},{5,1},{6,2},{7,3},{8,12},{9,13},{10,... | collective-permute-start | bytes 12296 | tf_op jit(solution)/shard_map/ppermute | solution.py:397
  85.5 3.9 %collective-permute-done = f32[8,128]{1,0:T(8,128)S(1)} collective-permute-done((f32[8,128]{1,0:T(8,128)S(1)}, f32[8,128]{1,0:T(8,128)S(1)}, u32[]{:S(2)}, u32[]{:S(2)}) %collective-permute-start) | collective-permute-done | bytes 4128 | tf_op jit(solution)/shard_map/ppermute | solution.py:397
  89.3 3.0 %collective-permute-start.1 = (f32[8,128]{1,0:T(8,128)S(1)}, f32[8,128]{1,0:T(8,128)S(1)}, u32[]{:S(2)}, u32[]{:S(2)}) collective-permute-start(f32[8,128]{1,0:T(8,128)S(1)} %max.9), channel_id=1, source_target_pairs={{0,2},{1,3},{2,0},{3,1},{4,6},{5,7},{6,4},{7,5},{8,10},{9,11},{10,... | collective-permute-start | bytes 12296 | tf_op jit(solution)/shard_map/ppermute | solution.py:397
  92.3 2.1 %collective-permute-done.1 = f32[8,128]{1,0:T(8,128)S(1)} collective-permute-done((f32[8,128]{1,0:T(8,128)S(1)}, f32[8,128]{1,0:T(8,128)S(1)}, u32[]{:S(2)}, u32[]{:S(2)}) %collective-permute-start.1) | collective-permute-done | bytes 4128 | tf_op jit(solution)/shard_map/ppermute | solution.py:397
  94.5 1.5 %collective-permute-start.2 = (f32[8,128]{1,0:T(8,128)S(1)}, f32[8,128]{1,0:T(8,128)S(1)}, u32[]{:S(2)}, u32[]{:S(2)}) collective-permute-start(f32[8,128]{1,0:T(8,128)S(1)} %max.10), channel_id=1, source_target_pairs={{0,1},{1,0},{2,3},{3,2},{4,5},{5,4},{6,7},{7,6},{8,9},{9,8},{10,11... | collective-permute-start | bytes 12296 | tf_op jit(solution)/shard_map/ppermute | solution.py:397
  95.9 2.1 %collective-permute-done.2 = f32[8,128]{1,0:T(8,128)S(1)} collective-permute-done((f32[8,128]{1,0:T(8,128)S(1)}, f32[8,128]{1,0:T(8,128)S(1)}, u32[]{:S(2)}, u32[]{:S(2)}) %collective-permute-start.2) | collective-permute-done | bytes 4128 | tf_op jit(solution)/shard_map/ppermute | solution.py:397
  98.1 0.5 slice.3
  98.6 0.0 all-to-all-done.1
  98.6 1.7 %copy_bitcast_fusion = bf16[8,3,64,768]{3,2,1,0:T(8,128)(2,1)} fusion(bf16[8,8,6,3,8,128]{5,4,3,2,1,0:T(8,128)(2,1)S(1)} %all-to-all-done.1), kind=kLoop, calls=%fused_computation.2 | loop fusion | bytes 4718592 | tf_op jit(solution)/shard_map/reshape | solution.py:393
  (11 shorter events, 0.1 us)
Async XLA Ops:
  0.6 26.0 %copy-start = (s32[64]{0:T(128)S(1)}, s32[64]{0:T(128)}, u32[]{:S(2)}) copy-start(s32[64]{0:T(128)} %param.12) | copy-start | bytes 772
  0.6 24.9 %copy-start.2 = (s32[1280]{0:T(1024)S(1)}, s32[1280]{0:T(1024)}, u32[]{:S(2)}) copy-start(s32[1280]{0:T(1024)} %all_waves.1) | copy-start | bytes 15364
  0.7 25.1 %copy-start.4 = (s32[48]{0:T(128)S(1)}, s32[48]{0:T(128)}, u32[]{:S(2)}) copy-start(s32[48]{0:T(128)} %param.13) | copy-start | bytes 580
  0.7 25.8 %copy-start.3 = (s32[128]{0:T(128)S(1)}, s32[128]{0:T(128)}, u32[]{:S(2)}) copy-start(s32[128]{0:T(128)} %param.11) | copy-start | bytes 1540
  19.0 23.8 %all-to-all-start = ((bf16[16,5,48,128]{3,2,1,0:T(8,128)(2,1)}), bf16[16,5,48,128]{3,2,1,0:T(8,128)(2,1)S(1)}, u32[]{:S(2)}, u32[]{:S(2)}) async-start(bf16[16,5,48,128]{3,2,1,0:T(8,128)(2,1)} %shard_map.86), calls=%async_computation | async-start | bytes 1966080 | tf_op jit(solution)/shard_map/all_to_all | solution.py:383
  34.3 4.0 %copy-start.1 = (bf16[8,256,2560]{2,1,0:T(8,128)(2,1)}, bf16[8,256,2560]{2,1,0:T(8,128)(2,1)S(1)}, u32[]{:S(2)}) copy-start(bf16[8,256,2560]{2,1,0:T(8,128)(2,1)S(1)} %get-tuple-element.6.table) | copy-start | bytes 31457284
  57.3 41.3 %all-to-all-start.1 = ((bf16[8,8,6,3,8,128]{5,4,3,2,1,0:T(8,128)(2,1)}), bf16[8,8,6,3,8,128]{5,4,3,2,1,0:T(8,128)(2,1)S(1)}, u32[]{:S(2)}, u32[]{:S(2)}) async-start(bf16[8,8,6,3,8,128]{5,4,3,2,1,0:T(8,128)(2,1)} %get-tuple-element.8), calls=%async_computation.1 | async-start | bytes 4718592 | tf_op jit(solution)/shard_map/all_to_all | solution.py:392
  84.0 5.4 %collective-permute-start = (f32[8,128]{1,0:T(8,128)S(1)}, f32[8,128]{1,0:T(8,128)S(1)}, u32[]{:S(2)}, u32[]{:S(2)}) collective-permute-start(f32[8,128]{1,0:T(8,128)S(1)} %bitcast_reduce_fusion), channel_id=1, source_target_pairs={{0,4},{1,5},{2,6},{3,7},{4,0},{5,1},{6,2},{7,3},{8,12},{9,13},{10,... | collective-permute-start | bytes 12296 | tf_op jit(solution)/shard_map/ppermute | solution.py:397
  89.3 5.1 %collective-permute-start.1 = (f32[8,128]{1,0:T(8,128)S(1)}, f32[8,128]{1,0:T(8,128)S(1)}, u32[]{:S(2)}, u32[]{:S(2)}) collective-permute-start(f32[8,128]{1,0:T(8,128)S(1)} %max.9), channel_id=1, source_target_pairs={{0,2},{1,3},{2,0},{3,1},{4,6},{5,7},{6,4},{7,5},{8,10},{9,11},{10,... | collective-permute-start | bytes 12296 | tf_op jit(solution)/shard_map/ppermute | solution.py:397
  94.5 3.6 %collective-permute-start.2 = (f32[8,128]{1,0:T(8,128)S(1)}, f32[8,128]{1,0:T(8,128)S(1)}, u32[]{:S(2)}, u32[]{:S(2)}) collective-permute-start(f32[8,128]{1,0:T(8,128)S(1)} %max.10), channel_id=1, source_target_pairs={{0,1},{1,0},{2,3},{3,2},{4,5},{5,4},{6,7},{7,6},{8,9},{9,8},{10,11... | collective-permute-start | bytes 12296 | tf_op jit(solution)/shard_map/ppermute | solution.py:397
